TPU v7x, 256 devices: a whole 4x4x8 slice. The times are simulated.
256 devices in a mesh: dp: 16 (over z, core), ctx: 16 (over y, x).
Axes of the slice: x: 4, y: 4, z: 8, core: 2. Of those that a mesh axis runs over, the one named last changes fastest.
Arguments:
- layer_input: bfloat16 [16, 4096, 2048], P('dp', 'ctx'), may hold values from -6 to 6
- proj_weight: bfloat16 [2048, 256], replicated, may hold values from -0.005859375 to 0.005859375
- ssd_input: bfloat16 [16, 4096, 2048], P('dp', 'ctx'), may hold values from -0.3125 to 0.3125
- log_decay: bfloat16 [16, 4096, 32], P('dp', 'ctx'), may hold values from -2 to 0
- segment_ids: int32 [16, 4096], P('dp', 'ctx'), may hold values from 0 to 3, never falling along the last dimension, each value on 1 to 2048 neighbouring positions
- ssd_cotangent: bfloat16 [16, 4096, 2048], P('dp', 'ctx'), may hold values from -6 to 6
- window_qkv: bfloat16 [16, 4096, 3, 1024], P('dp', 'ctx'), may hold values from -8 to 8
Outputs:
- ssd_input_grad: bfloat16 [16, 4096, 2048], P('dp', 'ctx')
- proj_out_grad: bfloat16 [16, 4096, 256], P('dp', 'ctx')
- proj_weight_grad: float32 [2048, 256], replicated
- window_out: bfloat16 [16, 4096, 1024], P('dp', 'ctx')
Inputs may be any that keep to these rules, and one draw needn't show every extreme that they name: `segment_ids`: within a sequence the ids never fall; each of the 4 documents holds 1 to 2048 tokens and one holds exactly 2048.
All inputs are finite; a program needn't handle non-finite values.
Results may differ from a plain program's by a relative error of at most 0.019.
Values may be sent and summed in bfloat16 or wider, within the bound.
No kernel may reach another device: no remote copies, remote signals or barrier semaphores. Data moves between devices by JAX's collectives and lax.ppermute only.
A program may use at most 192 MiB of HBM per device.

v0:
```python
import math

import jax
import jax.numpy as jnp
from jax import lax
from jax.sharding import PartitionSpec as P

STRETCH = 256
HEAD = 64
WIN = 2048


full_precision = lax.Precision.HIGHEST


def stretch_terms(inputs, cotangents, b_rows, c_rows, decays, segments, prev_seg):
    running = jnp.cumsum(decays, axis=0)
    final_sum = running[-1]
    to_end = jnp.where(
        (segments == segments[-1])[:, None], jnp.exp(final_sum[None, :] - running), 0.0
    )
    from_start = jnp.where((segments == prev_seg)[:, None], jnp.exp(running), 0.0)
    carry_gain = jnp.where(segments[-1] == prev_seg, jnp.exp(final_sum), 0.0)
    end_state = jnp.einsum("qn,qh,qhp->hnp", b_rows, to_end, inputs, precision=full_precision)
    start_grad = jnp.einsum(
        "qn,qh,qhp->hnp", c_rows, from_start, cotangents, precision=full_precision
    )
    return (carry_gain, end_state, start_grad)


def stretch_grads(
    inputs, cotangents, b_rows, c_rows, decays, segments, prev_seg, entering, leaving
):
    running = jnp.cumsum(decays, axis=0)
    final_sum = running[-1]
    to_end = jnp.where(
        (segments == segments[-1])[:, None], jnp.exp(final_sum[None, :] - running), 0.0
    )
    from_start = jnp.where((segments == prev_seg)[:, None], jnp.exp(running), 0.0)
    places = jnp.arange(segments.shape[0])
    allowed = (places[:, None] >= places[None, :]) & (segments[:, None] == segments[None, :])
    log_gap = running.T[:, :, None] - running.T[:, None, :]
    decay_mask = jnp.where(allowed[None], jnp.exp(jnp.where(allowed[None], log_gap, 0.0)), 0.0)
    c_dot_b = jnp.dot(c_rows, b_rows.T, precision=full_precision)
    dot_rows = jnp.einsum("thp,shp->hts", cotangents, inputs, precision=full_precision)
    mixed_sum = jnp.sum(decay_mask * dot_rows, axis=0)
    d_input = jnp.einsum(
        "hts,thp->shp", decay_mask * c_dot_b[None], cotangents, precision=full_precision
    )
    d_input = d_input + jnp.einsum(
        "sh,hnp,sn->shp", to_end, leaving, b_rows, precision=full_precision
    )
    grad_b = jnp.dot(mixed_sum.T, c_rows, precision=full_precision)
    grad_b = grad_b + jnp.einsum(
        "sh,hnp,shp->sn", to_end, leaving, inputs, precision=full_precision
    )
    grad_c = jnp.dot(mixed_sum, b_rows, precision=full_precision)
    grad_c = grad_c + jnp.einsum(
        "th,hnp,thp->tn", from_start, entering, cotangents, precision=full_precision
    )
    return (d_input, grad_b, grad_c)


def split_stretches(inputs, cotangents, b_rows, c_rows, decays, segments, prev_seg, block_len):
    length, head_count, head_width = inputs.shape
    block_count = length // block_len
    in_blocks = inputs.astype(jnp.float32).reshape(block_count, block_len, head_count, head_width)
    cot_blocks = cotangents.astype(jnp.float32).reshape(
        block_count, block_len, head_count, head_width
    )
    b_blocks = b_rows.astype(jnp.float32).reshape(block_count, block_len, -1)
    c_blocks = c_rows.astype(jnp.float32).reshape(block_count, block_len, -1)
    decay_blocks = decays.astype(jnp.float32).reshape(block_count, block_len, head_count)
    seg_blocks = segments.reshape(block_count, block_len)
    prev_segs = jnp.concatenate([jnp.reshape(prev_seg, (1,)), seg_blocks[:-1, -1]])
    return (in_blocks, cot_blocks, b_blocks, c_blocks, decay_blocks, seg_blocks, prev_segs)


def chain_before(carry_gain, end_state):

    def advance(carried, element):
        return (
            (carried[0] * element[0], element[0][:, None, None] * carried[1] + element[1]),
            carried,
        )

    starting = (jnp.ones_like(carry_gain[0]), jnp.zeros_like(end_state[0]))
    return lax.scan(advance, starting, (carry_gain, end_state))


def chain_after(carry_gain, start_grad):

    def advance(carried, element):
        return (
            (carried[0] * element[0], element[1] + element[0][:, None, None] * carried[1]),
            carried,
        )

    starting = (jnp.ones_like(carry_gain[0]), jnp.zeros_like(start_grad[0]))
    return lax.scan(advance, starting, (carry_gain, start_grad), reverse=True)


def stream_grads(pieces, before_pairs, after_pairs, entering, leaving):
    enter_all = before_pairs[1] + before_pairs[0][:, :, None, None] * entering[None]
    leave_all = after_pairs[1] + after_pairs[0][:, :, None, None] * leaving[None]

    def stream_per_block(element):
        return stretch_grads(*element)

    d_input, grad_b, grad_c = lax.map(stream_per_block, pieces + (enter_all, leave_all))
    block_count, block_len, head_count, head_width = pieces[0].shape
    total_rows = block_count * block_len
    return (
        d_input.reshape(total_rows, head_count, head_width),
        grad_b.reshape(total_rows, -1),
        grad_c.reshape(total_rows, -1),
    )


def masked_probs(scores, allowed):
    masked = jnp.where(allowed[None], scores, -jnp.inf)
    row_max = jnp.max(masked, axis=-1, keepdims=True)
    weights = jnp.exp(masked - row_max)
    return (weights / jnp.sum(weights, axis=-1, keepdims=True)).astype(jnp.bfloat16)


def window_attention(queries, key_rows, value_rows, seg_ids):
    length, head_count, head_width = queries.shape
    blocked = math.gcd(length, 512)
    lead_rows = jnp.zeros((WIN, head_count, head_width), jnp.bfloat16)
    padded_keys = jnp.concatenate([lead_rows, key_rows])
    padded_values = jnp.concatenate([lead_rows, value_rows])
    padded_ids = jnp.concatenate([jnp.full((WIN,), -1, jnp.int32), seg_ids])
    score_scale = head_width ** (-0.5)

    def window_per_block(offset):
        query_part = lax.dynamic_slice_in_dim(queries, offset, blocked, 0)
        key_part = lax.dynamic_slice_in_dim(padded_keys, offset, blocked + WIN, 0)
        value_part = lax.dynamic_slice_in_dim(padded_values, offset, blocked + WIN, 0)
        query_ids = lax.dynamic_slice_in_dim(seg_ids, offset, blocked, 0)
        key_ids = lax.dynamic_slice_in_dim(padded_ids, offset, blocked + WIN, 0)
        distance = (WIN + jnp.arange(blocked))[:, None] - jnp.arange(blocked + WIN)[None, :]
        allowed = (distance >= 0) & (distance < WIN) & (query_ids[:, None] == key_ids[None, :])
        scores = (
            jnp.einsum("qhe,khe->hqk", query_part, key_part, preferred_element_type=jnp.float32)
            * score_scale
        )
        weights = masked_probs(scores, allowed)
        return jnp.einsum(
            "hqk,khe->qhe", weights, value_part, preferred_element_type=jnp.float32
        ).astype(jnp.bfloat16)

    offsets = jnp.arange(length // blocked, dtype=jnp.int32) * blocked
    return lax.map(window_per_block, offsets).reshape(length, head_count, head_width)


def per_device(
    layer_input, proj_weight, ssd_input, log_decay, segment_ids, ssd_cotangent, window_qkv
):
    tok_rows = layer_input.shape[1]
    ctx_count = lax.axis_size("ctx")
    seq_len = tok_rows * ctx_count
    head_count = log_decay.shape[2]
    head_width = ssd_input.shape[2] // head_count
    gathered_ids = lax.all_gather(segment_ids, "ctx", axis=1, tiled=True)
    seq_ids = gathered_ids[0]
    projected = jnp.dot(layer_input[0], proj_weight, preferred_element_type=jnp.float32).astype(
        jnp.bfloat16
    )
    state_size = projected.shape[1] // 2
    local_heads = head_count // ctx_count
    ex_input, ex_cot, ex_decay = (
        lax.all_to_all(ssd_input, "ctx", split_axis=2, concat_axis=1, tiled=True),
        lax.all_to_all(ssd_cotangent, "ctx", split_axis=2, concat_axis=1, tiled=True),
        lax.all_to_all(log_decay, "ctx", split_axis=2, concat_axis=1, tiled=True),
    )
    all_proj = lax.all_gather(projected, "ctx", axis=0, tiled=True)
    pieces = split_stretches(
        ex_input[0].reshape(seq_len, local_heads, head_width),
        ex_cot[0].reshape(seq_len, local_heads, head_width),
        all_proj[:, :state_size],
        all_proj[:, state_size:],
        ex_decay[0],
        seq_ids,
        jnp.int32(-1),
        STRETCH,
    )
    carry_gain, end_state, start_grad = jax.vmap(stretch_terms)(*pieces)
    front_total, before_pairs = chain_before(carry_gain, end_state)
    back_total, after_pairs = chain_after(carry_gain, start_grad)
    no_state = jnp.zeros(end_state.shape[1:], jnp.float32)
    d_input, grad_b, grad_c = stream_grads(pieces, before_pairs, after_pairs, no_state, no_state)
    d_local = d_input.astype(jnp.bfloat16).reshape(1, seq_len, local_heads * head_width)
    input_grad = lax.all_to_all(d_local, "ctx", split_axis=1, concat_axis=2, tiled=True)
    partial_sums = jnp.concatenate([grad_b, grad_c], axis=1)
    out_grad = lax.psum_scatter(
        partial_sums.astype(jnp.bfloat16), "ctx", scatter_dimension=0, tiled=True
    )
    partial_value = jnp.einsum(
        "td,tn->dn", layer_input[0], out_grad, preferred_element_type=jnp.float32
    )
    token_total = lax.axis_size("dp") * seq_len
    weight_grad = lax.psum(partial_value, ("dp", "ctx")) / math.sqrt(token_total)
    exchanged = lax.all_to_all(window_qkv, "ctx", split_axis=3, concat_axis=1, tiled=True)
    attn_local = exchanged.shape[3] // HEAD
    qkv_rows = exchanged[0].reshape(seq_len, 3, attn_local, HEAD)
    attended = window_attention(qkv_rows[:, 0], qkv_rows[:, 1], qkv_rows[:, 2], seq_ids)
    window_out = lax.all_to_all(
        attended.reshape(1, seq_len, attn_local * HEAD),
        "ctx",
        split_axis=1,
        concat_axis=2,
        tiled=True,
    )
    return (input_grad, out_grad[None], weight_grad, window_out)


def solution(mesh):
    placed = (
        P("dp", "ctx", None),
        P(),
        P("dp", "ctx", None),
        P("dp", "ctx", None),
        P("dp", "ctx"),
        P("dp", "ctx", None),
        P("dp", "ctx", None, None),
    )
    return jax.shard_map(
        per_device,
        mesh=mesh,
        in_specs=placed,
        out_specs=(P("dp", "ctx", None), P("dp", "ctx", None), P(), P("dp", "ctx", None)),
        check_vma=False,
    )
```

profile of v0, /device:TPU:1, one launch (start us, length us, event | category | flops | bytes accessed | tf_op | source)
XLA Modules:
  0.0 1056.6 jit_solution(9584178604546900279)
XLA Ops:
  10.0 7.6 all-to-all-start.1
  17.6 4.6 copy.117
  22.2 11.6 %reduce.18 = bf16[2048,256]{1,0:T(8,128)(2,1)} reduce(bf16[2048,1,256]{2,1,0:T(2,128)(2,1)S(1)} %bitcast.327, bf16[]{:T(256)} %broadcast.200), dimensions={1}, to_apply=%bitcast.202.reduce_sub_computation | reduce | bytes 2097154
  33.8 2.3 reshape.285
  36.1 6.8 all-to-all-start.2
  44.2 25.5 %all_gather.6 = s32[1,4096]{1,0:T(1,128)S(1)} all-gather(s32[1,256]{1,0:T(1,128)S(1)} %copy-done.15), channel_id=1, replica_groups=mesh['dp'=16,'ctx'=16] {'ctx'}, dimensions={1}, use_global_device_ids=true | all-gather | bytes 17408 | tf_op jit(solution)/shard_map/all_gather | solution.py:165
  71.0 4.6 copy.104
  75.6 11.6 %reduce.16 = bf16[2048,256]{1,0:T(8,128)(2,1)} reduce(bf16[2048,1,256]{2,1,0:T(2,128)(2,1)S(1)} %bitcast.328, bf16[]{:T(256)} %broadcast.200), dimensions={1}, to_apply=%bitcast.198.reduce_sub_computation | reduce | bytes 2097154
  87.2 2.3 reshape.281
  89.5 2.6 copy.129
  93.4 4.4 all-to-all-start
  101.6 8.9 all-to-all-done
  110.5 4.4 all-to-all-start.4
  117.0 4.3 reshape.286
  123.7 5.8 reshape.282
  129.5 3.7 convert_bitcast_fusion.1
  134.7 4.1 all-to-all-done.4
  142.6 3.7 reshape_squeeze.9
  146.4 2.3 slice_bitcast_fusion.1
  150.6 2.6 fusion.91
  153.2 2.3 fusion.80
  157.1 71.3 %while.65 = (s32[]{:T(128)}, f32[2]{0:T(128)}, f32[2,128,64]{2,1,0:T(8,128)S(1)}, f32[16,2]{1,0:T(8,128)S(1)}, f32[16,2,128,64]{3,2,1,0:T(8,128)}, /*index=5*/f3...) while((s32[]{:T(128)}, f32[2]{0:T(128)}, f32[2,128,64]{2,1,0:T(8,128)S(1)}, ...), condition=%wide.region_3.4_spmd.clone, body=%wide.region_2.3_spmd.clone.sunk | while | flops 65543 | bytes 656053 | solution.py:88
  228.5 3.1 broadcast_add_fusion
  231.6 3.2 copy.125
  234.8 4.0 fusion.77
  240.4 39.3 %while.64 = (s32[]{:T(128)}, f32[2]{0:T(128)S(1)}, f32[2,128,64]{2,1,0:T(8,128)S(1)}, f32[16,2]{1,0:T(8,128)S(1)}, f32[16,2,128,64]{3,2,1,0:T(8,128)}, /*index=5...) while((s32[]{:T(128)}, f32[2]{0:T(128)S(1)}, ...), condition=%wide.region_5.6_spmd.clone, body=%wide.region_4.5_spmd.clone.sunk | while | flops 65544 | bytes 655565 | solution.py:100
  279.7 3.1 broadcast_add_fusion.1
  282.8 3.2 copy.124
  286.0 2.9 reshape.247
  290.5 348.7 %while.62 = (s32[]{:T(128)}, bf16[16,256,2,64]{1,3,2,0:T(8,128)(2,1)}, bf16[16,256,128]{2,1,0:T(8,128)(2,1)}, bf16[16,256,128]{2,1,0:T(8,128)(2,1)}, f32[16,256,...) while((s32[]{:T(128)}, ...), condition=%wide.region_10.11_spmd, body=%wide.region_6.10_spmd.sunk | while | flops 655886336 | bytes 4653929 | solution.py:110
  310.2 2.2 fusion.145
  353.8 2.2 fusion.145
  375.6 2.2 fusion.145
  397.4 2.2 fusion.145
  462.8 2.2 fusion.145
  484.5 2.2 fusion.145
  506.3 2.2 fusion.145
  549.9 2.2 fusion.145
  615.2 2.2 fusion.145
  637.0 2.2 fusion.145
  639.2 3.1 pad_maximum_fusion
  643.3 87.1 %while.63 = (s32[]{:T(128)}, bf16[8,512,1,64]{1,3,2,0:T(8,128)(2,1)S(1)}, s32[8]{0:T(128)S(1)}, bf16[6144,1,64]{0,2,1:T(8,128)(2,1)}, s32[4096]{0:T(1024)}, /*in...) while((s32[]{:T(128)}, ...), condition=%wide.region_16.17_spmd, body=%wide.region_13.16_spmd.sunk | while | flops 353926656 | bytes 16566992 | solution.py:154
  648.0 3.2 fusion.150
  658.9 3.2 fusion.150
  669.8 3.2 fusion.150
  680.7 3.2 fusion.150
  691.6 3.2 fusion.150
  702.5 3.2 fusion.150
  713.4 3.2 fusion.150
  724.3 3.2 fusion.150
  731.8 5.8 reshape.267
  737.6 23.7 %reduce.20 = bf16[4096,64]{1,0:T(8,128)(2,1)} reduce(bf16[4096,1,64]{2,1,0:T(2,128)(2,1)S(1)} %bitcast.326, bf16[]{:T(256)} %broadcast.200), dimensions={1}, to_apply=%bitcast.206.reduce_sub_computation | reduce | bytes 1048578
  761.2 3.0 reshape.289
  764.3 4.9 all-to-all-start.5
  769.2 2.7 convolution_bitcast_fusion.3
  772.0 4.0 copy.141
  776.0 7.7 reshape.266
  783.7 23.4 %reduce.19 = bf16[4096,128]{1,0:T(8,128)(2,1)} reduce(bf16[4096,1,128]{2,1,0:T(2,128)(2,1)S(1)} %bitcast.323, bf16[]{:T(256)} %broadcast.200), dimensions={1}, to_apply=%bitcast.204.reduce_sub_computation | reduce | bytes 2097154
  809.3 6.7 all-to-all-start.3
  816.0 4.1 reshape.290
  820.1 3.6 copy.134
  826.0 2.6 all-to-all-done.3
  828.7 4.3 reshape.288
  837.0 209.3 %all-reduce.5.cloned.1.call-done = f32[2048,256]{0,1:T(8,128)} async-done(((f32[2048,256]{0,1:T(8,128)}), f32[2048,256]{0,1:T(8,128)}) %all-reduce.5.cloned.1.call-update) | async-done | bytes 2097168 | tf_op jit(solution)/shard_map/psum | solution.py:203
  (785 shorter events, 511.9 us)
Async XLA Ops:
  7.2 35.8 %copy-start = (bf16[1,256,2048]{2,1,0:T(8,128)(2,1)S(1)}, bf16[1,256,2048]{2,1,0:T(8,128)(2,1)}, u32[]{:S(2)}) copy-start(bf16[1,256,2048]{2,1,0:T(8,128)(2,1)} %param.15) | copy-start | bytes 3145732
  10.0 26.1 %all-to-all-start.1 = ((bf16[16,2,256]{2,1,0:T(2,128)(2,1)}), bf16[16,2,256]{2,1,0:T(2,128)(2,1)S(1)}, u32[]{:S(2)}, u32[]{:S(2)}) async-start(bf16[16,2,256]{2,1,0:T(2,128)(2,1)} %reshape.283), calls=%async_computation.1 | async-start | bytes 32768 | tf_op jit(solution)/shard_map/all_to_all | solution.py:175
  33.8 9.2 copy-start.7
  36.1 8.1 copy-start.15
  36.1 57.3 %all-to-all-start.2 = ((bf16[16,2,16384]{2,1,0:T(2,128)(2,1)}), bf16[16,2,16384]{2,1,0:T(2,128)(2,1)}, u32[]{:S(2)}, u32[]{:S(2)}) async-start(bf16[16,2,16384]{2,1,0:T(2,128)(2,1)} %reshape.285), calls=%async_computation.2 | async-start | bytes 2097152 | tf_op jit(solution)/shard_map/all_to_all | solution.py:173
  42.9 107.6 %all-gather.2.cloned.1.call-start = ((), (), s32[]{:S(2)}) async-start(), calls=%async_computation.7 | async-start | bytes 2228224 | tf_op jit(solution)/shard_map/all_gather | solution.py:177
  69.8 22.3 %copy-start.10 = (s32[1,4096]{1,0:T(1,128)}, s32[1,4096]{1,0:T(1,128)S(1)}, u32[]{:S(2)}) copy-start(s32[1,4096]{1,0:T(1,128)S(1)} %all_gather.6) | copy-start | bytes 49156
  71.0 27.7 %copy-start.11 = (s32[16,256]{1,0:T(8,128)}, s32[16,256]{1,0:T(8,128)S(1)}, u32[]{:S(2)}) copy-start(s32[16,256]{1,0:T(8,128)S(1)} %reshape_squeeze.8) | copy-start | bytes 49156
  87.2 2.3 copy-start.5
  93.4 17.1 %all-to-all-start = ((bf16[16,2,16384]{2,1,0:T(2,128)(2,1)}), bf16[16,2,16384]{2,1,0:T(2,128)(2,1)S(1)}, u32[]{:S(2)}, u32[]{:S(2)}) async-start(bf16[16,2,16384]{2,1,0:T(2,128)(2,1)} %reshape.281), calls=%async_computation | async-start | bytes 2097152 | tf_op jit(solution)/shard_map/all_to_all | solution.py:174
  99.4 0.6 copy-start.12
  110.5 5.0 copy-start.3
  110.5 28.3 %all-to-all-start.4 = ((bf16[1,256,3,1024]{1,2,0,3:T(4,128)(2,1)}), bf16[1,256,3,1024]{1,2,0,3:T(4,128)(2,1)}, u32[]{:S(2)}, u32[]{:S(2)}) async-start(bf16[1,256,3,1024]{1,2,0,3:T(4,128)(2,1)} %copy.129), calls=%async_computation.5 | async-start | bytes 4194304 | tf_op jit(solution)/shard_map/all_to_all | solution.py:204
  114.9 654.3 %reduce-scatter.2.cloned.1.call-start = ((), (), s32[]{:S(2)}) async-start(), calls=%async_computation.8 | async-start | bytes 2228224 | tf_op jit(solution)/shard_map/reduce_scatter | solution.py:196
  153.2 2.3 copy-start.1
  231.6 3.2 copy-start.13
  238.7 1.7 copy-start.14
  286.0 2.9 copy-start.2
  299.7 3.8 copy-start.4
  321.5 3.8 copy-start.4
  343.3 3.8 copy-start.4
  365.1 3.8 copy-start.4
  386.9 3.8 copy-start.4
  408.7 3.8 copy-start.4
  430.5 3.8 copy-start.4
  452.3 3.8 copy-start.4
  474.0 3.8 copy-start.4
  495.8 3.8 copy-start.4
  517.6 3.8 copy-start.4
  539.4 3.8 copy-start.4
  561.2 3.8 copy-start.4
  582.9 3.8 copy-start.4
  604.7 3.8 copy-start.4
  626.5 3.8 copy-start.4
  642.3 1.0 copy-start.8
  642.3 1.0 copy-start.9
  642.3 1.0 copy-start.16
  764.3 45.0 %all-to-all-start.5 = ((bf16[16,2,8192]{2,1,0:T(2,128)(2,1)}), bf16[16,2,8192]{2,1,0:T(2,128)(2,1)}, u32[]{:S(2)}, u32[]{:S(2)}) async-start(bf16[16,2,8192]{2,1,0:T(2,128)(2,1)} %reshape.289), calls=%async_computation.6 | async-start | bytes 1048576 | tf_op jit(solution)/shard_map/all_to_all | solution.py:208
  769.2 2.9 copy-start.6
  769.2 277.1 %all-reduce.5.cloned.1.call-start = ((), (), s32[]{:S(2)}) async-start(), calls=%async_computation.9 | async-start | bytes 4194304 | tf_op jit(solution)/shard_map/psum | solution.py:203
  809.3 19.4 %all-to-all-start.3 = ((bf16[16,2,16384]{2,1,0:T(2,128)(2,1)}), bf16[16,2,16384]{2,1,0:T(2,128)(2,1)}, u32[]{:S(2)}, u32[]{:S(2)}) async-start(bf16[16,2,16384]{2,1,0:T(2,128)(2,1)} %reshape.287), calls=%async_computation.3 | async-start | bytes 2097152 | tf_op jit(solution)/shard_map/all_to_all | solution.py:194
Sparse Core Ops, SparseCore 0:
  46.8 53.0 all-gather.1
  642.4 83.8 reduce-scatter.1
  776.3 269.9 all-reduce.4
where the time goes:
time: 1080 us; the launch traced here: 1060 us
  matrix products  260 us (24%)
  local copies, waits for them, and re-layouts  252 us (23%)
  waiting for transfers between devices  225 us (21%)
  other arithmetic  216 us (20%)
  starting transfers between devices  35.5 us (3%)
  loops' own time  28.6 us (3%)
  blocking collectives  25.5 us (2%)
  between operations  14.4 us (1%)
    psum x1, waiting for transfers between devices, per_device(): lax.psum(partial_value, ('dp', 'ctx')) / math.sqrt(token_total)  209 us
    unnamed x9, other arithmetic  71.1 us
    dynamic_slice x80, local copies, waits for them, and re-layouts, chain_before(): return lax.scan(advance, starting, (carry_gain, end_state))  67 us
    unnamed x55, local copies, waits for them, and re-layouts  52.6 us
    dot_general x16, matrix products, stretch_grads(): jnp.einsum('hts,thp->shp', decay_mask * c_dot_b[None], cotangents, precis...  34.7 us
    dot_general x16, matrix products, stretch_grads(): grad_b = jnp.dot(mixed_sum.T, c_rows, precision=full_precision)  34.1 us
    mul x32, other arithmetic, advance(): carried[0] * element[0]  30.9 us
    dot_general x16, matrix products, stretch_grads(): grad_c = jnp.dot(mixed_sum, b_rows, precision=full_precision)  30.7 us
  transfers between devices with their start and end apart: 9, of which 4 were waited for; matrix products, arithmetic and copies ran while one was open for 22% of the time, Pallas kernels for 0%

commit v1 on v0

v1 whole, which is shorter than its diff:
```python
import math

import jax
import jax.numpy as jnp
from jax import lax
from jax.experimental import pallas as pl
from jax.experimental.pallas import tpu as pltpu
from jax.sharding import PartitionSpec as P

HEAD = 64
BIG = 16384.0
f32 = jnp.float32
bf16 = jnp.bfloat16
NT = (((1,), (1,)), ((), ()))


def mm(a, b):
    return jnp.dot(a, b, preferred_element_type=f32)


def mm_nt(a, b):
    return lax.dot_general(a, b, NT, preferred_element_type=f32)


def iota(shape, dim):
    return lax.broadcasted_iota(jnp.int32, shape, dim)


def ones_where(cond):
    return jnp.where(cond, 1.0, 0.0).astype(bf16)


def head_spread(heads, width, first):
    return ones_where(iota((heads, width), 0) == (iota((heads, width), 1) >> 6) + first)


def id_column(id_row):
    n = id_row.shape[1]
    eye = ones_where(iota((n, n), 0) == iota((n, n), 1))
    return mm_nt(eye, jnp.broadcast_to(id_row, (128, n)).astype(bf16))


def call(kernel, out_shape, *args, scratch=(), flops=0, n_bytes=4 << 20, prefetch=0):
    vmem = pl.BlockSpec(memory_space=pltpu.VMEM)
    smem = pl.BlockSpec(memory_space=pltpu.SMEM)
    many = isinstance(out_shape, (list, tuple))
    return pl.pallas_call(
        kernel,
        out_shape=out_shape,
        in_specs=[smem] * prefetch + [vmem] * (len(args) - prefetch),
        out_specs=[vmem] * len(out_shape) if many else vmem,
        scratch_shapes=list(scratch),
        compiler_params=pltpu.CompilerParams(vmem_limit_bytes=48 << 20),
        cost_estimate=pl.CostEstimate(flops=flops, bytes_accessed=n_bytes, transcendentals=0),
    )(*args)


def sds(shape, dtype):
    return jax.ShapeDtypeStruct(shape, dtype)


def states_kernel(inp, w, x, g, decay, ids, buf, proj_out, xs_out, gs_out, te_out):
    n_tok = inp.shape[0]
    heads = decay.shape[1]
    owners = buf.shape[0]
    proj = mm(inp[...], w[...]).astype(bf16)
    proj_out[...] = proj
    proj_t = proj.astype(f32).T.astype(bf16)
    half = proj.shape[1] // 2
    b_t, c_t = proj_t[:half], proj_t[half:]
    tri = ones_where(iota((n_tok, n_tok), 0) >= iota((n_tok, n_tok), 1))
    run = mm(tri, decay[...])
    final = run[n_tok - 1 : n_tok]
    id_row = ids[...].astype(f32)
    id_col = id_column(id_row)[:, :heads]
    first, last = id_col[:1], id_col[n_tok - 1 :]
    to_end = jnp.where(id_col == last, jnp.exp(final - run), 0.0).astype(bf16)
    from_start = jnp.where(id_col == first, jnp.exp(run), 0.0).astype(bf16)
    te_out[...] = to_end
    gain = jnp.where(first == last, jnp.exp(final), 0.0)
    gain_hi = gain.astype(bf16)
    gain_lo = (gain - gain_hi.astype(f32)).astype(bf16)
    gains = jnp.concatenate(
        [jnp.broadcast_to(gain_hi.astype(f32), (8, heads)), jnp.broadcast_to(gain_lo.astype(f32), (8, heads))]
    ).astype(bf16)
    row = iota((16, 128), 0)
    ends = jnp.where(row == 2, id_row[:, :1], id_row[:, n_tok - 1 :])
    for i in range(owners // 2):
        cols = slice(256 * i, 256 * i + 256)
        spread = head_spread(heads, 256, 4 * i)
        xs = (x[:, cols].astype(f32) * mm(to_end, spread)).astype(bf16)
        gs = (g[:, cols].astype(f32) * mm(from_start, spread)).astype(bf16)
        xs_out[:, cols] = xs
        gs_out[:, cols] = gs
        end_state = mm(b_t, xs).astype(bf16)
        start_grad = mm(c_t, gs).astype(bf16)
        gain_rows = mm(gains, spread)
        for k in range(2):
            part = slice(128 * k, 128 * k + 128)
            buf[2 * i + k, 0:128, :] = end_state[:, part]
            buf[2 * i + k, 128:256, :] = start_grad[:, part]
            meta = jnp.where(row == 0, gain_rows[0:1, part], jnp.where(row == 1, gain_rows[8:9, part], ends))
            buf[2 * i + k, 256:272, :] = meta.astype(bf16)


def chain_kernel(recv, send):
    count = recv.shape[0]
    meta = [recv[k, 256:272, :].astype(f32) for k in range(count)]
    gain = [m[0:1] + m[1:2] for m in meta]
    link = [jnp.zeros((1, 128), f32)]
    for k in range(1, count):
        link.append(jnp.where(meta[k][2:3] == meta[k - 1][3:4], 1.0, 0.0))
    state = jnp.zeros((128, 128), f32)
    for k in range(count):
        state = state * link[k]
        send[k, 0:128, :] = state.astype(bf16)
        state = state * gain[k] + recv[k, 0:128, :].astype(f32)
    adjoint = jnp.zeros((128, 128), f32)
    for k in range(count - 1, -1, -1):
        send[k, 128:256, :] = adjoint.astype(bf16)
        adjoint = (adjoint * gain[k] + recv[k, 128:256, :].astype(f32)) * link[k]


def intra_kernel(inp, proj, x, g, decay, ids, d_out, grad_out, inp_t, mixed):
    n_tok = inp.shape[0]
    heads = decay.shape[1]
    half = proj.shape[1] // 2
    square = (n_tok, n_tok)
    early, late = iota(square, 0), iota(square, 1)
    run = mm(ones_where(early >= late), decay[...])
    eye = ones_where(iota((heads, heads), 0) == iota((heads, heads), 1))
    decay_t = mm_nt(eye, decay[...]).astype(bf16)
    run_t = mm(decay_t, ones_where(early <= late))
    id_row = ids[...].astype(f32)
    id_col = id_column(id_row)[:, :1]
    bias = jnp.where((early <= late) & (id_col == id_row), 0.0, -1e30)
    b_rows, c_rows = proj[:, :half], proj[:, half:]
    b_dot_c = mm_nt(b_rows, c_rows)
    low_lane = iota((n_tok, 128), 1) < 64
    mixed[...] = jnp.zeros(square, f32)
    for p in range(heads // 2):
        cols = slice(128 * p, 128 * p + 128)
        xp, gp = x[:, cols], g[:, cols]
        zero = jnp.zeros_like(gp)
        total = jnp.zeros((n_tok, 128), f32)
        for k in range(2):
            h = 2 * p + k
            gh = jnp.where(low_lane, gp, zero) if k == 0 else jnp.where(low_lane, zero, gp)
            keep = jnp.exp(run_t[h : h + 1, :] - run[:, h : h + 1] + bias)
            mixed[...] += keep * mm_nt(xp, gh)
            total += mm((keep * b_dot_c).astype(bf16), gh)
        d_out[:, cols] = total
        inp_t[cols, :] = inp[:, cols].astype(f32).T.astype(bf16)
    both = mixed[...]
    grad_out[:, :half] = mm(both.astype(bf16), c_rows)
    grad_out[:, half:] = mm(both.T.astype(bf16), b_rows)


def outer_kernel(recv, xs, gs, grad_in, inp_t, og_out, share):
    owners = recv.shape[0]
    n_tok = xs.shape[0]
    grad_b = grad_in[:, :128]
    grad_c = grad_in[:, 128:]
    for i in range(owners // 2):
        cols = slice(256 * i, 256 * i + 256)
        enter = jnp.concatenate([recv[2 * i, 0:128, :], recv[2 * i + 1, 0:128, :]], axis=1)
        leave = jnp.concatenate([recv[2 * i, 128:256, :], recv[2 * i + 1, 128:256, :]], axis=1)
        grad_b += mm_nt(xs[:, cols], leave)
        grad_c += mm_nt(gs[:, cols], enter)
    og_out[:, :128] = grad_b.astype(bf16)
    og_out[:, 128:] = grad_c.astype(bf16)
    og = og_out[...]
    rows = inp_t.shape[0] // owners
    for j in range(owners):
        share[j] = mm(inp_t[rows * j : rows * j + rows, :], og).astype(bf16)


def input_grad_kernel(recv, proj, te, d_in, dx_out):
    owners = recv.shape[0]
    heads = te.shape[1]
    b_rows = proj[:, : proj.shape[1] // 2]
    for i in range(owners // 2):
        cols = slice(256 * i, 256 * i + 256)
        leave = jnp.concatenate([recv[2 * i, 128:256, :], recv[2 * i + 1, 128:256, :]], axis=1)
        spread = mm(te[...], head_spread(heads, 256, 4 * i))
        dx_out[:, cols] = (d_in[:, cols] + spread * mm(b_rows, leave)).astype(bf16)


def pack_kernel(qkv, ids, out):
    width = qkv.shape[1] // 3
    for m in range(3):
        for i in range(width // 128):
            at = m * width + 128 * i
            block = qkv[:, at : at + 128].astype(f32)
            if m == 0:
                block = block * HEAD ** (-0.5)
            turned = block.T.astype(bf16)
            out[2 * i, HEAD * m : HEAD * m + HEAD, :] = turned[:HEAD]
            out[2 * i + 1, HEAD * m : HEAD * m + HEAD, :] = turned[HEAD:]
    rows = jnp.broadcast_to(ids[...].astype(f32), (16, qkv.shape[0])).astype(bf16)
    for j in range(out.shape[0]):
        out[j, 192:208, :] = rows


def attention_kernel(lows, qkv, out, keys, values):
    blocks = qkv.shape[0]
    n = qkv.shape[2]
    slot = iota((16, n), 0).astype(f32)
    zeros48 = jnp.zeros((48, n), f32)
    pad_lane = iota((n, 128), 1)
    keys[0:n, :] = jnp.where((pad_lane >= 64) & (pad_lane < 80), -BIG, 0.0).astype(bf16)
    values[0] = jnp.zeros((80, n), bf16)

    def prepare(k, carry):
        ids = qkv[k, 192:208, :].astype(f32)
        other = jnp.where(ids == slot, 0.0, -BIG)
        tall = jnp.concatenate([qkv[k, 64:128, :].astype(f32), other, zeros48])
        keys[pl.ds(pl.multiple_of((k + 1) * n, n), n), :] = tall.T.astype(bf16)
        values[k + 1, 0:64, :] = qkv[k, 128:192, :]
        values[k + 1, 64:80, :] = jnp.ones((16, n), bf16)
        return carry

    lax.fori_loop(0, blocks, prepare, 0)
    future = jnp.where(iota((2 * n, n), 0) - n > iota((2 * n, n), 1), -BIG, 0.0)

    def per_block(b, carry):
        ids = qkv[b, 192:208, :].astype(f32)
        own = jnp.where(ids == slot, 1.0, 0.0)
        query = jnp.concatenate([qkv[b, 0:64, :].astype(f32), own, zeros48]).astype(bf16)

        def scores(at):
            return mm(keys[pl.ds(pl.multiple_of(at * n, n), 2 * n), :], query)

        def weighted(at, p):
            return mm(values[at], p[:n]) + mm(values[at + 1], p[n:])

        s = scores(b) + future
        top = jnp.max(s, axis=0, keepdims=True)
        total = weighted(b, jnp.exp(s - top).astype(bf16))

        def step(i, held):
            top, total = held
            at = b - 2 * i
            s = scores(at)
            new_top = jnp.maximum(top, jnp.max(s, axis=0, keepdims=True))
            p = jnp.exp(s - new_top).astype(bf16)
            return new_top, total * jnp.exp(top - new_top) + weighted(at, p)

        pairs = (b + 2 - lows[b]) // 2
        top, total = lax.fori_loop(1, pairs, step, (top, total))
        out[b] = (total[0:64] / total[64:65]).astype(bf16)
        return carry

    lax.fori_loop(0, blocks, per_block, 0)


def unpack_kernel(recv, out):
    for i in range(recv.shape[0] // 2):
        tall = jnp.concatenate([recv[2 * i], recv[2 * i + 1]]).astype(f32)
        out[:, 128 * i : 128 * i + 128] = tall.T.astype(bf16)


def exchange(blocks, axis):
    return lax.all_to_all(blocks, axis, split_axis=0, concat_axis=0, tiled=True)


def per_device(layer_input, proj_weight, ssd_input, log_decay, segment_ids, ssd_cotangent, window_qkv):
    inp, x, g = layer_input[0], ssd_input[0], ssd_cotangent[0]
    decay = log_decay[0]
    n_tok, width = inp.shape
    heads = decay.shape[1]
    ctx = lax.axis_size("ctx")
    dp = lax.axis_size("dp")
    n_out = proj_weight.shape[1]

    buf, proj, xs, gs, te = call(
        states_kernel,
        (
            sds((ctx, 272, 128), bf16),
            sds((n_tok, n_out), bf16),
            sds((n_tok, width), bf16),
            sds((n_tok, width), bf16),
            sds((n_tok, heads), bf16),
        ),
        inp, proj_weight, x, g, decay, segment_ids,
        flops=2 << 30, n_bytes=9 << 20,
    )
    got = exchange(buf, "ctx")

    packed = call(
        pack_kernel,
        sds((ctx, 208, n_tok), bf16),
        window_qkv.reshape(n_tok, -1), segment_ids,
        n_bytes=8 << 20,
    )
    rows = exchange(packed, "ctx")

    d_intra, grad_intra, inp_t = call(
        intra_kernel,
        (sds((n_tok, width), f32), sds((n_tok, n_out), f32), sds((width, n_tok), bf16)),
        inp, proj, x, g, decay, segment_ids,
        scratch=[pltpu.VMEM((n_tok, n_tok), f32)],
        flops=6 << 30, n_bytes=8 << 20,
    )
    back = exchange(call(chain_kernel, sds((ctx, 256, 128), bf16), got, n_bytes=6 << 20), "ctx")

    ids = rows[:, 192, :].astype(jnp.int32)
    lows = jnp.sum(ids[None, :, -1] < ids[:, None, 0], axis=1, dtype=jnp.int32)
    attended = call(
        attention_kernel,
        sds((ctx, HEAD, n_tok), bf16),
        lows, rows,
        scratch=[pltpu.VMEM(((ctx + 1) * n_tok, 128), bf16), pltpu.VMEM((ctx + 1, 80, n_tok), bf16)],
        flops=16 << 30, n_bytes=2 << 20, prefetch=1,
    )
    out_rows = exchange(attended, "ctx")

    out_grad, share = call(
        outer_kernel,
        (sds((n_tok, n_out), bf16), sds((ctx, width // ctx, n_out), bf16)),
        back, xs, gs, grad_intra, inp_t,
        flops=2 << 30, n_bytes=6 << 20,
    )
    shares = exchange(share, "ctx")
    part = jnp.sum(shares.astype(f32), axis=0).astype(bf16)
    parts = exchange(part.reshape(dp, -1, n_out), "dp")
    own = jnp.sum(parts.astype(f32), axis=0).astype(bf16)
    strip = exchange(jnp.broadcast_to(own[None], (dp,) + own.shape), "dp").reshape(part.shape)
    whole = exchange(jnp.broadcast_to(strip[None], (ctx,) + strip.shape), "ctx")
    weight_grad = whole.reshape(width, n_out).astype(f32) / math.sqrt(dp * ctx * n_tok)

    input_grad = call(
        input_grad_kernel, sds((n_tok, width), bf16), back, proj, te, d_intra, flops=1 << 30, n_bytes=4 << 20
    )
    window_out = call(unpack_kernel, sds((n_tok, ctx * HEAD), bf16), out_rows, n_bytes=1 << 20)
    return (input_grad[None], out_grad[None], weight_grad, window_out[None])


def solution(mesh):
    placed = (
        P("dp", "ctx", None),
        P(),
        P("dp", "ctx", None),
        P("dp", "ctx", None),
        P("dp", "ctx"),
        P("dp", "ctx", None),
        P("dp", "ctx", None, None),
    )
    return jax.shard_map(
        per_device,
        mesh=mesh,
        in_specs=placed,
        out_specs=(P("dp", "ctx", None), P("dp", "ctx", None), P(), P("dp", "ctx", None)),
        check_vma=False,
    )
```

time: 1080 us -> 195 us (0.18); the launches traced: 1060 us -> 195 us
  matrix products: 260 us -> 0 us
  local copies, waits for them, and re-layouts: 252 us -> 15.8 us
  other arithmetic: 216 us -> 3.36 us
  waiting for transfers between devices: 225 us -> 60.4 us
  Pallas kernels: 0 us -> 41.2 us
  loops' own time: 28.6 us -> 0 us
  blocking collectives: 25.5 us -> 39.6 us
  between operations: 14.4 us -> 0.77 us
    dot_general x132 -> x0, matrix products: 241 us -> none  [the longest x16 34.7 us: stretch_grads(): jnp.einsum('hts,thp->shp', decay_mask * c_dot_b[None], cotangents, precis...]
    psum x1 -> x0, waiting for transfers between devices: 209 us -> none  [per_device(): lax.psum(partial_value, ('dp', 'ctx')) / math.sqrt(token_total)]
    dynamic_slice x136 -> x0, local copies, waits for them, and re-layouts: 109 us -> none  [the longest x80 67 us: chain_before(): return lax.scan(advance, starting, (carry_gain, end_state))]
    unnamed x9 -> x0, other arithmetic: 71.1 us -> none
    all_to_all x6, waiting for transfers between devices: 15.6 us -> 60.4 us  [exchange(): return lax.all_to_all(blocks, axis, split_axis=0, concat_axis=0, tiled=True)]
    pallas_call x0 -> x8, Pallas kernels: none -> 41.2 us  [call(): pl.pallas_call(kernel, out_shape=out_shape, in_specs=[smem] * prefetch +...]
    unnamed x55 -> x31, local copies, waits for them, and re-layouts: 52.6 us -> 12.8 us
    all_to_all x0 -> x2, blocking collectives: none -> 39.6 us  [exchange(): return lax.all_to_all(blocks, axis, split_axis=0, concat_axis=0, tiled=True)]
  transfers between devices with their start and end apart: 9 -> 6, of which waited for: 4 -> 5; matrix products, arithmetic and copies ran while one was open for 22% -> 2% of each run, Pallas kernels for 0% -> 18%
where the time goes in v1:
time: 195 us
  waiting for transfers between devices  60.4 us (31%)
  Pallas kernels  41.2 us (21%)
  blocking collectives  39.6 us (20%)
  starting transfers between devices  33.6 us (17%)
  local copies, waits for them, and re-layouts  15.8 us (8%)
  other arithmetic  3.36 us (2%)
    all_to_all x6, waiting for transfers between devices, exchange(): return lax.all_to_all(blocks, axis, split_axis=0, concat_axis=0, tiled=True)  60.4 us
    pallas_call x8, Pallas kernels, call(): pl.pallas_call(kernel, out_shape=out_shape, in_specs=[smem] * prefetch +...  41.2 us
    all_to_all x2, blocking collectives, exchange(): return lax.all_to_all(blocks, axis, split_axis=0, concat_axis=0, tiled=True)  39.6 us
    all_to_all x6, starting transfers between devices, exchange(): return lax.all_to_all(blocks, axis, split_axis=0, concat_axis=0, tiled=True)  33.6 us
    unnamed x31, local copies, waits for them, and re-layouts  12.8 us
  transfers between devices with their start and end apart: 6, of which 5 were waited for; matrix products, arithmetic and copies ran while one was open for 2% of the time, Pallas kernels for 18%

profile of v1, /device:TPU:1, one launch (start us, length us, event | category | flops | bytes accessed | tf_op | source)
XLA Modules:
  0.0 194.7 jit_solution(10732029078339155445)
XLA Ops:
  0.6 0.8 copy.16
  1.5 0.0 copy-start.1
  1.5 0.7 copy-done.1
  2.1 0.0 copy-start.3
  2.2 1.2 copy-done.3
  3.4 0.0 copy-start.4
  3.4 1.2 copy-done.4
  4.6 0.0 copy-start.6
  4.6 1.2 copy-done.6
  5.8 4.8 %shard_map.102 = (bf16[16,272,128]{2,1,0:T(8,128)(2,1)}, bf16[256,256]{1,0:T(8,128)(2,1)S(1)}, bf16[256,2048]{1,0:T(8,128)(2,1)S(1)}, bf16[256,2048]{1,0:T(8,128)(2,1)S(1)}, bf16[256,32]{1,0:T(8,128)(2,1)S(1)}) custom-call(bf16[256,2048]{1,0:T(8,128)(2,1)S(1)} %bitcast.16, bf16[2048,256]{1,0:T(8,128)(2,1)S(1)} %copy-done.3, bf16[256,2048]{1,0:T(8,128)(2,1)S(1)} %bitcast.18, ...), custom_call_target="tpu_custom_call" | custom-call | flops 2147483648 | bytes 9437184 | tf_op jit(solution)/shard_map/pallas_call | solution.py:47
  10.6 0.0 copy-start.9
  10.6 1.0 copy-done.9
  11.6 0.0 copy-start.11
  11.6 1.0 copy-done.11
  12.6 24.5 %all_to_all.40.recv = bf16[16,272,128]{2,1,0:T(8,128)(2,1)S(1)} all-to-all(bf16[16,272,128]{2,1,0:T(8,128)(2,1)} %get-tuple-element.14), channel_id=1, replica_groups=mesh['dp'=16,'ctx'=16] {'ctx'}, dimensions={0} | all-to-all | bytes 2228224 | tf_op jit(solution)/shard_map/all_to_all | solution.py:264
  37.1 0.0 copy-start.13
  37.1 1.3 shard_map.103
  38.4 3.7 %all-to-all-start.1 = ((bf16[16,256,128]{2,1,0:T(8,128)(2,1)}), bf16[16,256,128]{2,1,0:T(8,128)(2,1)S(1)}, u32[]{:S(2)}, u32[]{:S(2)}) async-start(bf16[16,256,128]{2,1,0:T(8,128)(2,1)} %shard_map.103), calls=%async_computation.1 | async-start | bytes 2097152 | tf_op jit(solution)/shard_map/all_to_all | solution.py:264
  42.0 0.0 copy-done.13
  42.0 1.6 copy.17
  43.6 0.0 copy-start.2
  43.6 1.7 copy.18.qkv
  45.3 0.0 copy-done.2
  45.3 1.7 shard_map.107
  47.0 0.0 copy-start.5
  47.0 10.1 %all-to-all-done.1.recv = bf16[16,256,128]{2,1,0:T(8,128)(2,1)S(1)} async-done(((bf16[16,256,128]{2,1,0:T(8,128)(2,1)}), bf16[16,256,128]{2,1,0:T(8,128)(2,1)S(1)}, u32[]{:S(2)}, u32[]{:S(2)}) %all-to-all-start.1) | async-done | bytes 1048608 | tf_op jit(solution)/shard_map/all_to_all | solution.py:264
  57.1 5.0 %all-to-all-start.6 = ((bf16[16,208,256]{2,1,0:T(8,128)(2,1)}), bf16[16,208,256]{2,1,0:T(8,128)(2,1)}, u32[]{:S(2)}, u32[]{:S(2)}) async-start(bf16[16,208,256]{2,1,0:T(8,128)(2,1)} %shard_map.107), calls=%async_computation.6 | async-start | bytes 3407872 | tf_op jit(solution)/shard_map/all_to_all | solution.py:264
  62.1 0.0 copy-done.5
  62.1 0.0 copy-start.7
  62.1 1.2 copy-done.7
  63.3 0.0 copy-start.8
  63.3 1.2 copy-done.8
  64.6 0.0 copy-start.10
  64.6 0.0 copy-start.12
  64.6 5.1 %shard_map.104 = (f32[256,2048]{1,0:T(8,128)}, f32[256,256]{1,0:T(8,128)S(1)}, bf16[2048,256]{1,0:T(8,128)(2,1)S(1)}) custom-call(bf16[256,2048]{1,0:T(8,128)(2,1)S(1)} %bitcast.17, bf16[256,256]{1,0:T(8,128)(2,1)S(1)} %get-tuple-element.15.proj, bf16[256,2048]{1,0:T(8,128)(2,1)S(1)} %bitcast.19, bf16[256,2048]{1,0:T(8,128)(2,1)S(1)} %bitcast.21, ...), custom_call_target="tpu_custom_call" | custom-call | flops 6442450944 | bytes 8388608 | tf_op jit(solution)/shard_map/pallas_call | solution.py:47
  69.6 0.0 copy-done.10
  69.6 0.0 copy-done.12
  69.7 2.1 %shard_map.106 = (bf16[256,256]{1,0:T(8,128)(2,1)}, bf16[16,128,256]{2,1,0:T(8,128)(2,1)}) custom-call(bf16[16,256,128]{2,1,0:T(8,128)(2,1)S(1)} %all-to-all-done.1.recv, bf16[256,2048]{1,0:T(8,128)(2,1)S(1)} %copy-done.10, bf16[256,2048]{1,0:T(8,128)(2,1)S(1)} %copy-done.12, f32[256,256]{1,0:T(8,128)S(1)} %get-tuple-element.20.grad_in, ...), custom_call_target="tpu_custom_call" | custom-call | flops 2147483648 | bytes 6291456 | tf_op jit(solution)/shard_map/pallas_call | solution.py:47
  71.8 11.7 %all-to-all-done.6.qkv = bf16[16,208,256]{2,1,0:T(8,128)(2,1)} async-done(((bf16[16,208,256]{2,1,0:T(8,128)(2,1)}), bf16[16,208,256]{2,1,0:T(8,128)(2,1)}, u32[]{:S(2)}, u32[]{:S(2)}) %all-to-all-start.6) | async-done | bytes 1703968 | tf_op jit(solution)/shard_map/all_to_all | solution.py:264
  83.5 5.7 %all-to-all-start.2 = ((bf16[16,128,256]{2,1,0:T(8,128)(2,1)}), bf16[16,128,256]{2,1,0:T(8,128)(2,1)S(1)}, u32[]{:S(2)}, u32[]{:S(2)}) async-start(bf16[16,128,256]{2,1,0:T(8,128)(2,1)} %get-tuple-element.23), calls=%async_computation.2 | async-start | bytes 2097152 | tf_op jit(solution)/shard_map/all_to_all | solution.py:264
  89.2 0.9 slice_convert_fusion
  90.1 0.2 slice_reduce_fusion
  90.2 0.2 convert_reduce_fusion.lows
  90.4 13.7 %all-to-all-done.2 = bf16[16,128,256]{2,1,0:T(8,128)(2,1)S(1)} async-done(((bf16[16,128,256]{2,1,0:T(8,128)(2,1)}), bf16[16,128,256]{2,1,0:T(8,128)(2,1)S(1)}, u32[]{:S(2)}, u32[]{:S(2)}) %all-to-all-start.2) | async-done | bytes 1048608 | tf_op jit(solution)/shard_map/all_to_all | solution.py:264
  104.1 0.8 reduce_sum.33
  104.9 12.1 %all-to-all-start.3 = ((bf16[16,8,256]{2,1,0:T(8,128)(2,1)}), bf16[16,8,256]{2,1,0:T(8,128)(2,1)S(1)}, u32[]{:S(2)}, u32[]{:S(2)}) async-start(bf16[16,8,256]{2,1,0:T(8,128)(2,1)} %bitcast.6), calls=%async_computation.3 | async-start | bytes 131072 | tf_op jit(solution)/shard_map/all_to_all | solution.py:264
  116.9 23.6 %shard_map.108 = bf16[16,64,256]{2,1,0:T(8,128)(2,1)} custom-call(s32[16]{0:T(128)S(1)} %convert_reduce_fusion.lows, bf16[16,208,256]{2,1,0:T(8,128)(2,1)} %all-to-all-done.6.qkv), custom_call_target="tpu_custom_call" | custom-call | flops 17179869184 | bytes 2097152 | tf_op jit(solution)/shard_map/pallas_call | solution.py:47
  140.5 0.0 all-to-all-done.3
  140.6 3.6 %all-to-all-start.7 = ((bf16[16,64,256]{2,1,0:T(8,128)(2,1)}), bf16[16,64,256]{2,1,0:T(8,128)(2,1)S(1)}, u32[]{:S(2)}, u32[]{:S(2)}) async-start(bf16[16,64,256]{2,1,0:T(8,128)(2,1)} %shard_map.108), calls=%async_computation.7 | async-start | bytes 1048576 | tf_op jit(solution)/shard_map/all_to_all | solution.py:264
  144.2 10.8 %all-to-all-done.7.recv = bf16[16,64,256]{2,1,0:T(8,128)(2,1)S(1)} async-done(((bf16[16,64,256]{2,1,0:T(8,128)(2,1)}), bf16[16,64,256]{2,1,0:T(8,128)(2,1)S(1)}, u32[]{:S(2)}, u32[]{:S(2)}) %all-to-all-start.7) | async-done | bytes 524320 | tf_op jit(solution)/shard_map/all_to_all | solution.py:264
  155.0 15.1 %all_to_all.41 = bf16[16,8,256]{2,1,0:T(8,128)(2,1)S(1)} all-to-all(bf16[16,8,256]{2,1,0:T(8,128)(2,1)S(1)} %broadcast_in_dim.24), channel_id=1, replica_groups=mesh['dp'=16,'ctx'=16] {'dp'}, dimensions={0} | all-to-all | bytes 131072 | tf_op jit(solution)/shard_map/all_to_all | solution.py:264
  170.1 1.1 broadcast_in_dim.26
  171.1 3.7 %all-to-all-start.5 = ((bf16[16,128,256]{2,1,0:T(8,128)(2,1)}), bf16[16,128,256]{2,1,0:T(8,128)(2,1)S(1)}, u32[]{:S(2)}, u32[]{:S(2)}) async-start(bf16[16,128,256]{2,1,0:T(8,128)(2,1)} %broadcast_in_dim.26), calls=%async_computation.5 | async-start | bytes 2097152 | tf_op jit(solution)/shard_map/all_to_all | solution.py:264
  174.8 0.0 copy-start
  174.8 1.6 copy-done
  176.4 1.7 shard_map.105
  178.1 1.0 shard_map.109
  179.1 14.1 %all-to-all-done.5 = bf16[16,128,256]{2,1,0:T(8,128)(2,1)S(1)} async-done(((bf16[16,128,256]{2,1,0:T(8,128)(2,1)}), bf16[16,128,256]{2,1,0:T(8,128)(2,1)S(1)}, u32[]{:S(2)}, u32[]{:S(2)}) %all-to-all-start.5) | async-done | bytes 1048608 | tf_op jit(solution)/shard_map/all_to_all | solution.py:264
  193.2 1.5 convert_multiply_fusion
  (3 shorter events, 0.0 us)
Async XLA Ops:
  1.5 0.7 copy-start.1
  2.1 1.2 copy-start.3
  3.4 1.2 copy-start.4
  4.6 1.2 copy-start.6
  10.6 1.0 copy-start.9
  11.6 1.0 copy-start.11
  37.1 4.9 %copy-start.13 = (bf16[1,256,3,1024]{3,1,2,0:T(8,128)(2,1)S(1)}, bf16[1,256,3,1024]{3,1,2,0:T(8,128)(2,1)}, u32[]{:S(2)}) copy-start(bf16[1,256,3,1024]{3,1,2,0:T(8,128)(2,1)} %param.13) | copy-start | bytes 4718596
  38.4 18.7 %all-to-all-start.1 = ((bf16[16,256,128]{2,1,0:T(8,128)(2,1)}), bf16[16,256,128]{2,1,0:T(8,128)(2,1)S(1)}, u32[]{:S(2)}, u32[]{:S(2)}) async-start(bf16[16,256,128]{2,1,0:T(8,128)(2,1)} %shard_map.103), calls=%async_computation.1 | async-start | bytes 2097152 | tf_op jit(solution)/shard_map/all_to_all | solution.py:264
  43.6 1.7 copy-start.2
  47.0 15.1 %copy-start.5 = (bf16[1,256,2048]{2,1,0:T(8,128)(2,1)S(1)}, bf16[1,256,2048]{2,1,0:T(8,128)(2,1)}, u32[]{:S(2)}) copy-start(bf16[1,256,2048]{2,1,0:T(8,128)(2,1)} %param.7) | copy-start | bytes 3145732
  57.1 26.4 %all-to-all-start.6 = ((bf16[16,208,256]{2,1,0:T(8,128)(2,1)}), bf16[16,208,256]{2,1,0:T(8,128)(2,1)}, u32[]{:S(2)}, u32[]{:S(2)}) async-start(bf16[16,208,256]{2,1,0:T(8,128)(2,1)} %shard_map.107), calls=%async_computation.6 | async-start | bytes 3407872 | tf_op jit(solution)/shard_map/all_to_all | solution.py:264
  62.1 1.2 copy-start.7
  63.3 1.2 copy-start.8
  64.6 5.1 %copy-start.10 = (bf16[256,2048]{1,0:T(8,128)(2,1)S(1)}, bf16[256,2048]{1,0:T(8,128)(2,1)}, u32[]{:S(2)}) copy-start(bf16[256,2048]{1,0:T(8,128)(2,1)} %copy-done.9) | copy-start | bytes 3145732
  64.6 5.1 %copy-start.12 = (bf16[256,2048]{1,0:T(8,128)(2,1)S(1)}, bf16[256,2048]{1,0:T(8,128)(2,1)}, u32[]{:S(2)}) copy-start(bf16[256,2048]{1,0:T(8,128)(2,1)} %copy-done.11) | copy-start | bytes 3145732
  83.5 20.6 %all-to-all-start.2 = ((bf16[16,128,256]{2,1,0:T(8,128)(2,1)}), bf16[16,128,256]{2,1,0:T(8,128)(2,1)S(1)}, u32[]{:S(2)}, u32[]{:S(2)}) async-start(bf16[16,128,256]{2,1,0:T(8,128)(2,1)} %get-tuple-element.23), calls=%async_computation.2 | async-start | bytes 2097152 | tf_op jit(solution)/shard_map/all_to_all | solution.py:264
  104.9 35.7 %all-to-all-start.3 = ((bf16[16,8,256]{2,1,0:T(8,128)(2,1)}), bf16[16,8,256]{2,1,0:T(8,128)(2,1)S(1)}, u32[]{:S(2)}, u32[]{:S(2)}) async-start(bf16[16,8,256]{2,1,0:T(8,128)(2,1)} %bitcast.6), calls=%async_computation.3 | async-start | bytes 131072 | tf_op jit(solution)/shard_map/all_to_all | solution.py:264
  140.6 14.4 %all-to-all-start.7 = ((bf16[16,64,256]{2,1,0:T(8,128)(2,1)}), bf16[16,64,256]{2,1,0:T(8,128)(2,1)S(1)}, u32[]{:S(2)}, u32[]{:S(2)}) async-start(bf16[16,64,256]{2,1,0:T(8,128)(2,1)} %shard_map.108), calls=%async_computation.7 | async-start | bytes 1048576 | tf_op jit(solution)/shard_map/all_to_all | solution.py:264
  171.1 22.1 %all-to-all-start.5 = ((bf16[16,128,256]{2,1,0:T(8,128)(2,1)}), bf16[16,128,256]{2,1,0:T(8,128)(2,1)S(1)}, u32[]{:S(2)}, u32[]{:S(2)}) async-start(bf16[16,128,256]{2,1,0:T(8,128)(2,1)} %broadcast_in_dim.26), calls=%async_computation.5 | async-start | bytes 2097152 | tf_op jit(solution)/shard_map/all_to_all | solution.py:264
  174.8 1.6 copy-start

commit v2 on v1

v2 whole, which is shorter than its diff:
```python
import functools
import math

import jax
import jax.numpy as jnp
from jax import lax
from jax.experimental import pallas as pl
from jax.experimental.pallas import tpu as pltpu
from jax.sharding import PartitionSpec as P

HEAD = 64
BIG = 16384.0
f32 = jnp.float32
bf16 = jnp.bfloat16
NT = (((1,), (1,)), ((), ()))


def mm(a, b):
    return jnp.dot(a, b, preferred_element_type=f32)


def mm_nt(a, b):
    return lax.dot_general(a, b, NT, preferred_element_type=f32)


def iota(shape, dim):
    return lax.broadcasted_iota(jnp.int32, shape, dim)


def ones_where(cond):
    return jnp.where(cond, 1.0, 0.0).astype(bf16)


def head_spread(heads, width, first):
    return ones_where(iota((heads, width), 0) == (iota((heads, width), 1) >> 6) + first)


def id_column(id_row):
    n = id_row.shape[1]
    eye = ones_where(iota((n, n), 0) == iota((n, n), 1))
    return mm_nt(eye, jnp.broadcast_to(id_row, (128, n)).astype(bf16))


def call(kernel, out_shape, *args, scratch=(), flops=0, n_bytes=4 << 20, prefetch=0, limit=24 << 20, hbm=(), out_hbm=False):
    vmem = pl.BlockSpec(memory_space=pltpu.VMEM)
    smem = pl.BlockSpec(memory_space=pltpu.SMEM)
    any_hbm = pl.BlockSpec(memory_space=pltpu.HBM)
    many = isinstance(out_shape, (list, tuple))
    return pl.pallas_call(
        kernel,
        out_shape=out_shape,
        in_specs=[smem if k < prefetch else any_hbm if k in hbm else vmem for k in range(len(args))],
        out_specs=[vmem] * len(out_shape) if many else any_hbm if out_hbm else vmem,
        scratch_shapes=list(scratch),
        compiler_params=pltpu.CompilerParams(vmem_limit_bytes=limit),
        cost_estimate=pl.CostEstimate(flops=flops, bytes_accessed=n_bytes, transcendentals=0),
    )(*args)


def sds(shape, dtype):
    return jax.ShapeDtypeStruct(shape, dtype)


def front_kernel(
    inp_hbm, w_hbm, x_hbm, g_hbm, qkv_hbm, decay_hbm, ids_hbm,
    buf_hbm, proj_out, te_out, fs_out,
    inp, w, x, g, qkv, decay_t, ids, buf, in_sem, part_sem, out_sem,
):
    n_tok, width = inp.shape
    heads = decay_t.shape[0]
    owners = buf.shape[0]
    whole = [
        pltpu.make_async_copy(src, dst, in_sem.at[k])
        for k, (src, dst) in enumerate(
            [(decay_hbm, decay_t), (ids_hbm, ids)]
            + [(qkv_hbm.at[m], qkv.at[m]) for m in range(3)]
            + [
                (src.at[:, pl.ds(width // 4 * q, width // 4)], dst.at[:, pl.ds(width // 4 * q, width // 4)])
                for q in range(4)
                for src, dst in ((x_hbm, x), (g_hbm, g))
            ]
        )
    ]
    chunk = width // 4
    parts = []
    for k in range(4):
        at = pl.ds(chunk * k, chunk)
        parts.append(
            (
                pltpu.make_async_copy(inp_hbm.at[:, at], inp.at[:, at], part_sem.at[0, k]),
                pltpu.make_async_copy(w_hbm.at[at, :], w.at[at, :], part_sem.at[1, k]),
            )
        )
    whole[0].start()
    whole[1].start()
    for pair in parts:
        pair[0].start()
        pair[1].start()
    for copy in whole[5:] + whole[2:5]:
        copy.start()

    early, late = iota((n_tok, n_tok), 0), iota((n_tok, n_tok), 1)
    tri = ones_where(early >= late)
    whole[0].wait()
    whole[1].wait()
    run = mm_nt(tri, decay_t[...])
    final = run[n_tok - 1 : n_tok]
    id_row = ids[...].astype(f32)
    id_col = id_column(id_row)[:, :heads]
    first, last = id_col[:1], id_col[n_tok - 1 :]
    to_end = jnp.where(id_col == last, jnp.exp(final - run), 0.0).astype(bf16)
    from_start = jnp.where(id_col == first, jnp.exp(run), 0.0).astype(bf16)
    te_out[...] = to_end
    fs_out[...] = from_start
    gain = jnp.where(first == last, jnp.exp(final), 0.0)
    gain_hi = gain.astype(bf16)
    gain_lo = (gain - gain_hi.astype(f32)).astype(bf16)
    gains = jnp.concatenate(
        [jnp.broadcast_to(gain_hi.astype(f32), (8, heads)), jnp.broadcast_to(gain_lo.astype(f32), (8, heads))]
    ).astype(bf16)
    row = iota((16, 256), 0)
    ends = jnp.where(row == 0, id_row, jnp.where(row == 3, id_row[:, :1], id_row[:, n_tok - 1 :]))

    total = jnp.zeros((n_tok, w.shape[1]), f32)
    for k in range(4):
        at = slice(chunk * k, chunk * k + chunk)
        parts[k][0].wait()
        parts[k][1].wait()
        total += mm(inp[:, at], w[at, :])
    proj = total.astype(bf16)
    proj_out[...] = proj
    proj_t = proj.astype(f32).T.astype(bf16)
    half = proj.shape[1] // 2
    b_t, c_t = proj_t[:half], proj_t[half:]
    sends = []
    for i in range(owners // 2):
        if i % 2 == 0:
            whole[5 + i].wait()
            whole[6 + i].wait()
        cols = slice(256 * i, 256 * i + 256)
        spread = head_spread(heads, 256, 4 * i)
        xs = (x[:, cols].astype(f32) * mm(to_end, spread)).astype(bf16)
        gs = (g[:, cols].astype(f32) * mm(from_start, spread)).astype(bf16)
        end_state = mm(b_t, xs).astype(bf16)
        start_grad = mm(c_t, gs).astype(bf16)
        gain_rows = mm(gains, spread)
        for k in range(2):
            part = slice(128 * k, 128 * k + 128)
            buf[2 * i + k, 0:128, 0:128] = end_state[:, part]
            buf[2 * i + k, 0:128, 128:256] = start_grad[:, part]
            gain_hi_row = jnp.concatenate([gain_rows[0:1, part]] * 2, axis=1)
            gain_lo_row = jnp.concatenate([gain_rows[8:9, part]] * 2, axis=1)
            meta = jnp.where(row == 1, gain_hi_row, jnp.where(row == 2, gain_lo_row, ends))
            buf[2 * i + k, 128:144, :] = meta.astype(bf16)
        span = (pl.ds(2 * i, 2), pl.ds(0, 144))
        sends.append(pltpu.make_async_copy(buf.at[span], buf_hbm.at[span], out_sem.at[0, i]))
        sends[-1].start()
    for m in range(3):
        whole[2 + m].wait()
    for i in range(owners // 2):
        for m in range(3):
            block = qkv[m, :, 128 * i : 128 * i + 128].astype(f32)
            if m == 0:
                block = block * HEAD ** (-0.5)
            turned = block.T.astype(bf16)
            at = slice(144 + HEAD * m, 144 + HEAD * m + HEAD)
            buf[2 * i, at, :] = turned[:HEAD]
            buf[2 * i + 1, at, :] = turned[HEAD:]
        span = (pl.ds(2 * i, 2), pl.ds(144, 192))
        sends.append(pltpu.make_async_copy(buf.at[span], buf_hbm.at[span], out_sem.at[1, i]))
        sends[-1].start()
    for copy in sends:
        copy.wait()


def chain_kernel(recv, after, send_hbm, send, sem):
    count = recv.shape[0]
    meta = [recv[k, 128:144, :].astype(f32) for k in range(count)]
    gain = [m[1:2, :128] + m[2:3, :128] for m in meta]
    link = [jnp.zeros((1, 128), f32)]
    for k in range(1, count):
        link.append(jnp.where(meta[k][3:4, :128] == meta[k - 1][4:5, :128], 1.0, 0.0))
    state = jnp.zeros((128, 128), f32)
    for k in range(count):
        state = state * link[k]
        send[k, :, 0:128] = state.astype(bf16)
        state = state * gain[k] + recv[k, 0:128, 0:128].astype(f32)
    adjoint = jnp.zeros((128, 128), f32)
    copies = []
    for k in range(count - 1, -1, -1):
        send[k, :, 128:256] = adjoint.astype(bf16)
        copies.append(pltpu.make_async_copy(send.at[k], send_hbm.at[k], sem.at[k]))
        copies[-1].start()
        adjoint = (adjoint * gain[k] + recv[k, 0:128, 128:256].astype(f32)) * link[k]
    for copy in copies:
        copy.wait()


def intra_kernel(inp, proj, x, g, te, fs, decay_t, ids, d_out, grad_out, kept, done, mixed):
    done[...] = jnp.zeros(done.shape, f32)
    n_tok = inp.shape[0]
    heads = decay_t.shape[0]
    half = proj.shape[1] // 2
    square = (n_tok, n_tok)
    early, late = iota(square, 0), iota(square, 1)
    run = mm_nt(ones_where(early >= late), decay_t[...])
    run_t = mm(decay_t[...], ones_where(early <= late))
    id_row = ids[...].astype(f32)
    id_col = id_column(id_row)[:, :1]
    bias = jnp.where((early <= late) & (id_col == id_row), 0.0, -1e30)
    b_rows, c_rows = proj[:, :half], proj[:, half:]
    b_dot_c = mm_nt(b_rows, c_rows)
    low_lane = iota((n_tok, 128), 1) < 64
    mixed[...] = jnp.zeros(square, f32)
    for p in range(heads // 2):
        cols = slice(128 * p, 128 * p + 128)
        xp, gp = x[:, cols], g[:, cols]
        zero = jnp.zeros_like(gp)
        total = jnp.zeros((n_tok, 128), f32)
        for k in range(2):
            h = 2 * p + k
            gh = jnp.where(low_lane, gp, zero) if k == 0 else jnp.where(low_lane, zero, gp)
            keep = jnp.exp(run_t[h : h + 1, :] - run[:, h : h + 1] + bias)
            mixed[...] += keep * mm_nt(xp, gh)
            total += mm((keep * b_dot_c).astype(bf16), gh)
        d_out[:, cols] = total
        spread = head_spread(heads, 128, 2 * p)
        rows = slice(n_tok * (p // 2), n_tok * (p // 2) + n_tok)
        side = slice(128 * (p % 2), 128 * (p % 2) + 128)
        kept[0, rows, side] = (xp.astype(f32) * mm(te[...], spread)).astype(bf16)
        kept[1, rows, side] = (gp.astype(f32) * mm(fs[...], spread)).astype(bf16)
        kept[2, cols, :] = inp[:, cols].astype(f32).T.astype(bf16)
    both = mixed[...]
    grad_out[:, :half] = mm(both.astype(bf16), c_rows)
    grad_out[:, half:] = mm(both.T.astype(bf16), b_rows)


def outer_kernel(core, recv_hbm, kept_hbm, grad_in, after, og_out, keep, give, recv, kept, sem):
    owners = recv.shape[0]
    n_tok = grad_in.shape[0]
    copies, arrivals = [], []
    for q in range(4):
        rows = pl.ds(kept.shape[1] // 4 * q, kept.shape[1] // 4)
        for k in range(2):
            copies.append(pltpu.make_async_copy(kept_hbm.at[k, rows], kept.at[k, rows], sem.at[2 * q + k]))
        span = pl.ds(owners // 4 * q, owners // 4)
        arrivals.append(pltpu.make_async_copy(recv_hbm.at[span], recv.at[span], sem.at[9 + q]))
        arrivals[-1].start()
        copies[2 * q].start()
        copies[2 * q + 1].start()
    copies.append(pltpu.make_async_copy(kept_hbm.at[2], kept.at[2], sem.at[8]))
    copies[8].start()
    grad_b = grad_in[:, :128]
    grad_c = grad_in[:, 128:]
    for i in range(owners // 2):
        if i % 2 == 0:
            copies[i].wait()
            copies[i + 1].wait()
            arrivals[i // 2].wait()
        rows = slice(n_tok * i, n_tok * i + n_tok)
        enter = jnp.concatenate([recv[2 * i, :, 0:128], recv[2 * i + 1, :, 0:128]], axis=1)
        leave = jnp.concatenate([recv[2 * i, :, 128:256], recv[2 * i + 1, :, 128:256]], axis=1)
        grad_b += mm_nt(kept[0, rows, :], leave)
        grad_c += mm_nt(kept[1, rows, :], enter)
    og_out[:, :128] = grad_b.astype(bf16)
    og_out[:, 128:] = grad_c.astype(bf16)
    og = og_out[...]
    copies[8].wait()
    rows = kept.shape[1] // owners // 2
    mine = pl.multiple_of(core[0] * rows, rows)
    other = pl.multiple_of(rows - core[0] * rows, rows)
    for j in range(owners):
        keep[j] = mm(kept[2, pl.ds(2 * rows * j + mine, rows), :], og)
        give[j] = mm(kept[2, pl.ds(2 * rows * j + other, rows), :], og).astype(bf16)


def input_grad_kernel(recv, proj, te, d_in, dx_out, done):
    done[...] = jnp.zeros(done.shape, f32)
    owners = recv.shape[0]
    heads = te.shape[1]
    b_rows = proj[:, : proj.shape[1] // 2]
    for i in range(owners // 2):
        cols = slice(256 * i, 256 * i + 256)
        leave = jnp.concatenate([recv[2 * i, :, 128:256], recv[2 * i + 1, :, 128:256]], axis=1)
        spread = mm(te[...], head_spread(heads, 256, 4 * i))
        dx_out[:, cols] = (d_in[:, cols] + spread * mm(b_rows, leave)).astype(bf16)


def attention_kernel(lows, qkv, out, done, keys, values):
    done[...] = jnp.zeros(done.shape, f32)
    blocks = qkv.shape[0]
    n = qkv.shape[2]
    slot = iota((16, n), 0).astype(f32)
    zeros48 = jnp.zeros((48, n), f32)

    def prepare(k, carry):
        ids = qkv[k, 128:144, :].astype(f32)[0:1]
        other = jnp.where(ids == slot, 0.0, -BIG)
        tall = jnp.concatenate([qkv[k, 208:272, :].astype(f32), other, zeros48])
        keys[pl.ds(pl.multiple_of(k * n, n), n), :] = tall.T.astype(bf16)
        values[k, 0:64, :] = qkv[k, 272:336, :]
        values[k, 64:80, :] = jnp.ones((16, n), bf16)
        return carry

    lax.fori_loop(0, blocks, prepare, 0)
    later = iota((2 * n, n), 0) - iota((2 * n, n), 1)
    masks = [jnp.where(later > k * n, -BIG, 0.0) for k in range(2)]

    def per_pair(c, carry):
        queries = []
        for k in range(2):
            ids = qkv[2 * c + k, 128:144, :].astype(f32)[0:1]
            own = jnp.where(ids == slot, 1.0, 0.0)
            rows = qkv[2 * c + k, 144:208, :].astype(f32)
            queries.append(jnp.concatenate([rows, own, zeros48]).astype(bf16))

        def scores(at, query):
            return mm(keys[pl.ds(pl.multiple_of(at * n, n), 2 * n), :], query)

        def weighted(at, p):
            return mm(values[at], p[:n]) + mm(values[at + 1], p[n:])

        held = []
        for k in range(2):
            s = scores(2 * c, queries[k]) + masks[k]
            top = jnp.max(s, axis=0, keepdims=True)
            held += [top, weighted(2 * c, jnp.exp(s - top).astype(bf16))]

        def step(i, held):
            at = 2 * (c - i)
            new = []
            s = [scores(at, query) for query in queries]
            for k in range(2):
                top, total = held[2 * k], held[2 * k + 1]
                new_top = jnp.maximum(top, jnp.max(s[k], axis=0, keepdims=True))
                p = jnp.exp(s[k] - new_top).astype(bf16)
                new += [new_top, total * jnp.exp(top - new_top) + weighted(at, p)]
            return tuple(new)

        held = lax.fori_loop(1, c + 1 - lows[2 * c] // 2, step, tuple(held))
        for k in range(2):
            total = held[2 * k + 1]
            out[2 * c + k] = (total[0:64] / total[64:65]).astype(bf16)
        return carry

    lax.fori_loop(0, blocks // 2, per_pair, 0)


def unpack_kernel(recv, out, done):
    done[...] = jnp.zeros(done.shape, f32)
    for i in range(recv.shape[0] // 2):
        tall = jnp.concatenate([recv[2 * i, 64:128], recv[2 * i + 1, 64:128]]).astype(f32)
        out[:, 128 * i : 128 * i + 128] = tall.T.astype(bf16)


def sum_kernel(recv, after, out):
    rows = out.shape[1]
    total = recv[0, 0:rows, :].astype(f32)
    for k in range(1, recv.shape[0]):
        total += recv[k, 0:rows, :].astype(f32)
    total = total.astype(bf16)
    for k in range(out.shape[0]):
        out[k] = total


def assemble_kernel(core, mine, other, out, *, scale):
    for j in range(out.shape[0]):
        out[j, core[0]] = mine[j].astype(f32) * scale
        out[j, 1 - core[0]] = other[j].astype(f32) * scale


def exchange(blocks, axis, groups=None):
    return lax.all_to_all(blocks, axis, split_axis=0, concat_axis=0, tiled=True, axis_index_groups=groups)


def per_device(layer_input, proj_weight, ssd_input, log_decay, segment_ids, ssd_cotangent, window_qkv):
    inp, x, g = layer_input[0], ssd_input[0], ssd_cotangent[0]
    decay_t = log_decay[0].T
    qkv = window_qkv[0].transpose(1, 0, 2)
    n_tok, width = inp.shape
    heads = decay_t.shape[0]
    ctx = lax.axis_size("ctx")
    dp = lax.axis_size("dp")
    n_out = proj_weight.shape[1]
    core = lax.axis_index("dp") % 2
    pairs = [(i, i ^ 1) for i in range(dp)]
    planes = [list(range(c, dp, 2)) for c in range(2)]

    done = sds((8, 128), f32)

    vmem = pl.BlockSpec(memory_space=pltpu.VMEM)
    anywhere = pl.BlockSpec(memory_space=pltpu.HBM)
    buf, proj, te, fs = pl.pallas_call(
        front_kernel,
        out_shape=(
            sds((ctx, 336, n_tok), bf16),
            sds((n_tok, n_out), bf16),
            sds((n_tok, heads), bf16),
            sds((n_tok, heads), bf16),
        ),
        in_specs=[anywhere] * 7,
        out_specs=(anywhere, vmem, vmem, vmem),
        scratch_shapes=[
            pltpu.VMEM(a.shape, a.dtype) for a in (inp, proj_weight, x, g, qkv, decay_t, segment_ids)
        ]
        + [
            pltpu.VMEM((ctx, 336, n_tok), bf16),
            pltpu.SemaphoreType.DMA((13,)),
            pltpu.SemaphoreType.DMA((2, 4)),
            pltpu.SemaphoreType.DMA((2, ctx // 2)),
        ],
        compiler_params=pltpu.CompilerParams(vmem_limit_bytes=64 << 20),
        cost_estimate=pl.CostEstimate(flops=2 << 30, bytes_accessed=9 << 20, transcendentals=0),
    )(inp, proj_weight, x, g, qkv, decay_t, segment_ids)
    got = exchange(buf, "ctx")

    d_intra, grad_intra, kept, intra_done = call(
        intra_kernel,
        (
            sds((n_tok, width), f32),
            sds((n_tok, n_out), f32),
            sds((3, width, n_tok), bf16),
            done,
        ),
        inp, proj, x, g, te, fs, decay_t, segment_ids,
        scratch=[pltpu.VMEM((n_tok, n_tok), f32)],
        flops=6 << 30, n_bytes=8 << 20,
    )
    sent = call(
        chain_kernel,
        sds((ctx, 128, 256), bf16),
        got, intra_done,
        scratch=[pltpu.VMEM((ctx, 128, 256), bf16), pltpu.SemaphoreType.DMA((ctx,))],
        n_bytes=6 << 20, limit=24 << 20, out_hbm=True,
    )
    back = exchange(sent, "ctx")

    ids = got[:, 128, :].astype(jnp.int32)
    lows = jnp.sum(ids[None, :, -1] < ids[:, None, 0], axis=1, dtype=jnp.int32)
    attended, attention_done = call(
        attention_kernel,
        (sds((ctx, HEAD, n_tok), bf16), done),
        lows, got,
        scratch=[pltpu.VMEM((ctx * n_tok, 128), bf16), pltpu.VMEM((ctx, 80, n_tok), bf16)],
        flops=16 << 30, n_bytes=2 << 20, prefetch=1,
    )

    half_rows = width // ctx // 2
    out_grad, keep, give = call(
        outer_kernel,
        (sds((n_tok, n_out), bf16), sds((ctx, half_rows, n_out), f32), sds((ctx, half_rows, n_out), bf16)),
        core[None], back, kept, grad_intra, attention_done,
        scratch=[
            pltpu.VMEM((ctx, 128, 256), bf16),
            pltpu.VMEM((3, width, n_tok), bf16),
            pltpu.SemaphoreType.DMA((13,)),
        ],
        flops=2 << 30, n_bytes=6 << 20, prefetch=1, limit=62 << 20, hbm=(1, 2),
    )
    share = (keep + lax.ppermute(give, "dp", pairs).astype(f32)).astype(bf16)
    third = exchange(jnp.concatenate([share, attended], axis=1), "ctx")
    input_grad, input_done = call(
        input_grad_kernel,
        (sds((n_tok, width), bf16), done),
        back, proj, te, d_intra,
        flops=1 << 30, n_bytes=4 << 20,
    )
    part = call(sum_kernel, sds((dp // 2, half_rows, n_out), bf16), third, input_done, n_bytes=2 << 20)
    parts = exchange(part, "dp", planes)
    window_out, window_done = call(
        unpack_kernel, (sds((n_tok, ctx * HEAD), bf16), done), third, n_bytes=1 << 20
    )
    strip = call(sum_kernel, sds((ctx, half_rows, n_out), bf16), parts, window_done, n_bytes=1 << 20)
    mine = exchange(strip, "ctx")
    other = lax.ppermute(mine, "dp", pairs)
    weight_grad = call(
        functools.partial(assemble_kernel, scale=1.0 / math.sqrt(dp * ctx * n_tok)),
        sds((ctx, 2, half_rows, n_out), f32),
        core[None], mine, other,
        n_bytes=4 << 20, prefetch=1,
    ).reshape(width, n_out)
    return (input_grad[None], out_grad[None], weight_grad, window_out[None])


def solution(mesh):
    placed = (
        P("dp", "ctx", None),
        P(),
        P("dp", "ctx", None),
        P("dp", "ctx", None),
        P("dp", "ctx"),
        P("dp", "ctx", None),
        P("dp", "ctx", None, None),
    )
    return jax.shard_map(
        per_device,
        mesh=mesh,
        in_specs=placed,
        out_specs=(P("dp", "ctx", None), P("dp", "ctx", None), P(), P("dp", "ctx", None)),
        check_vma=False,
    )
```

time: 195 us -> 157 us (0.81)
  blocking collectives: 39.6 us -> 14.9 us
  local copies, waits for them, and re-layouts: 15.8 us -> 9.11 us
  waiting for transfers between devices: 60.4 us -> 53.9 us
    all_to_all x2 -> x1, blocking collectives: 39.6 us -> 14.9 us  [exchange(): lax.all_to_all(blocks, axis, split_axis=0, concat_axis=0, tiled=True, axi...]
    all_to_all x6 -> x4, waiting for transfers between devices: 60.4 us -> 50.7 us  [exchange(): lax.all_to_all(blocks, axis, split_axis=0, concat_axis=0, tiled=True, axi...]
    ppermute x0 -> x2, starting transfers between devices: none -> 5.1 us  [the longest x1 3.18 us: per_device(): other = lax.ppermute(mine, 'dp', pairs)]
    all_to_all x6 -> x4, starting transfers between devices: 33.6 us -> 28.9 us  [exchange(): lax.all_to_all(blocks, axis, split_axis=0, concat_axis=0, tiled=True, axi...]
    unnamed x31 -> x29, local copies, waits for them, and re-layouts: 12.8 us -> 8.93 us
    ppermute x0 -> x2, waiting for transfers between devices: none -> 3.28 us  [the longest x1 1.75 us: per_device(): share = (keep + lax.ppermute(give, 'dp', pairs).astype(f32)).astype(bf16)]
    pallas_call x8 -> x10, Pallas kernels: 41.2 us -> 41.6 us  [the longest x9 33.8 us: call(): pl.pallas_call(kernel, out_shape=out_shape, in_specs=[smem if k < prefetc...]
  transfers between devices with their start and end apart: 6 -> 6, of which waited for: 5 -> 5; matrix products, arithmetic and copies ran while one was open for 2% -> 0% of each run, Pallas kernels for 18% -> 16%
where the time goes in v2:
time: 157 us
  waiting for transfers between devices  53.9 us (34%)
  Pallas kernels  41.6 us (26%)
  starting transfers between devices  34 us (22%)
  blocking collectives  14.9 us (9%)
  local copies, waits for them, and re-layouts  9.11 us (6%)
  other arithmetic  2.64 us (2%)
    all_to_all x4, waiting for transfers between devices, exchange(): lax.all_to_all(blocks, axis, split_axis=0, concat_axis=0, tiled=True, axi...  50.7 us
    pallas_call x9, Pallas kernels, call(): pl.pallas_call(kernel, out_shape=out_shape, in_specs=[smem if k < prefetc...  33.8 us
    all_to_all x4, starting transfers between devices, exchange(): lax.all_to_all(blocks, axis, split_axis=0, concat_axis=0, tiled=True, axi...  28.9 us
    all_to_all x1, blocking collectives, exchange(): lax.all_to_all(blocks, axis, split_axis=0, concat_axis=0, tiled=True, axi...  14.9 us
    unnamed x29, local copies, waits for them, and re-layouts  8.93 us
    pallas_call x1, Pallas kernels, per_device(): pl.pallas_call(front_kernel, out_shape=(sds((ctx, 336, n_tok), bf16), sds...  7.8 us
    ppermute x1, starting transfers between devices, per_device(): other = lax.ppermute(mine, 'dp', pairs)  3.18 us
  transfers between devices with their start and end apart: 6, of which 5 were waited for; matrix products, arithmetic and copies ran while one was open for 0% of the time, Pallas kernels for 16%

profile of v2, /device:TPU:1, one launch (start us, length us, event | category | flops | bytes accessed | tf_op | source)
XLA Modules:
  0.0 157.0 jit_solution(12670310362499394018)
XLA Ops:
  0.6 7.8 %shard_map.102 = (bf16[16,336,256]{2,1,0:T(8,128)(2,1)}, bf16[256,256]{1,0:T(8,128)(2,1)}, bf16[256,32]{1,0:T(8,128)(2,1)}, bf16[256,32]{1,0:T(8,128)(2,1)}) custom-call(bf16[256,2048]{1,0:T(8,128)(2,1)} %bitcast.17, bf16[2048,256]{1,0:T(8,128)(2,1)} %w_hbm.1, bf16[256,2048]{1,0:T(8,128)(2,1)} %bitcast.19, bf16[256,2048]{1,0:T(8,128)(2,1)} %bitcast.21, ...), custom_call_target="tpu_custom_call" | custom-call | flops 2147483648 | bytes 9437184 | tf_op jit(solution)/shard_map/pallas_call | solution.py:393
  8.4 0.0 copy-start.4
  8.4 0.0 copy-start.5
  8.5 0.0 copy-start.8
  8.5 0.0 copy-start.10
  8.5 0.0 copy-start.12
  8.5 7.7 %all-to-all-start = ((bf16[16,336,256]{2,1,0:T(8,128)(2,1)}), bf16[16,336,256]{2,1,0:T(8,128)(2,1)S(1)}, u32[]{:S(2)}, u32[]{:S(2)}) async-start(bf16[16,336,256]{2,1,0:T(8,128)(2,1)} %get-tuple-element.21), calls=%async_computation | async-start | bytes 5505024 | tf_op jit(solution)/shard_map/all_to_all | solution.py:373
  16.2 0.0 copy-done.4
  16.2 0.0 copy-done.5
  16.3 0.0 copy-done.8
  16.3 0.0 copy-done.10
  16.3 0.0 copy-done.12
  16.3 0.0 copy-start.1
  16.3 1.2 copy-done.1
  17.5 0.0 copy-start.2
  17.5 1.2 copy-done.2
  18.7 0.0 copy-start.3
  18.7 1.2 copy-done.3
  20.0 4.5 %shard_map.103 = (f32[256,2048]{1,0:T(8,128)S(1)}, f32[256,256]{1,0:T(8,128)S(1)}, bf16[3,2048,256]{2,1,0:T(8,128)(2,1)S(1)}, f32[8,128]{1,0:T(8,128)S(1)}) custom-call(bf16[256,2048]{1,0:T(8,128)(2,1)S(1)} %bitcast.18, bf16[256,256]{1,0:T(8,128)(2,1)S(1)} %copy-done.8, bf16[256,2048]{1,0:T(8,128)(2,1)S(1)} %bitcast.20, bf16[256,2048]{1,0:T(8,128)(2,1)S(1)} %bitcast.22, ...), custom_call_target="tpu_custom_call" | custom-call | flops 6442450944 | bytes 8388608 | tf_op jit(solution)/shard_map/pallas_call | solution.py:49
  24.5 0.0 copy-start.6
  24.5 1.3 copy-done.6
  25.8 0.0 copy-start.9
  25.8 1.6 %copy-done.9 = bf16[3,2048,256]{2,1,0:T(8,128)(2,1)} copy-done((bf16[3,2048,256]{2,1,0:T(8,128)(2,1)}, bf16[3,2048,256]{2,1,0:T(8,128)(2,1)S(1)}, u32[]{:S(2)}) %copy-start.9) | copy-done | bytes 3145752
  27.5 0.0 copy-start.11
  27.5 0.7 copy-done.11
  28.2 28.8 %all-to-all-done.recv.qkv = bf16[16,336,256]{2,1,0:T(8,128)(2,1)S(1)} async-done(((bf16[16,336,256]{2,1,0:T(8,128)(2,1)}), bf16[16,336,256]{2,1,0:T(8,128)(2,1)S(1)}, u32[]{:S(2)}, u32[]{:S(2)}) %all-to-all-start) | async-done | bytes 2752544 | tf_op jit(solution)/shard_map/all_to_all | solution.py:373
  57.0 0.2 slice_reduce_fusion
  57.2 1.9 %shard_map.104 = bf16[16,128,256]{2,1,0:T(8,128)(2,1)S(1)} custom-call(bf16[16,336,256]{2,1,0:T(8,128)(2,1)S(1)} %all-to-all-done.recv.qkv, f32[8,128]{1,0:T(8,128)S(1)} %get-tuple-element.25.after), custom_call_target="tpu_custom_call" | custom-call | bytes 6291456 | tf_op jit(solution)/shard_map/pallas_call | solution.py:49
  59.1 0.0 copy-start
  59.1 1.0 copy-done
  60.1 4.3 %all-to-all-start.1 = ((bf16[16,128,256]{2,1,0:T(8,128)(2,1)}), bf16[16,128,256]{2,1,0:T(8,128)(2,1)}, u32[]{:S(2)}, u32[]{:S(2)}) async-start(bf16[16,128,256]{2,1,0:T(8,128)(2,1)} %copy-done), calls=%async_computation.1 | async-start | bytes 2097152 | tf_op jit(solution)/shard_map/all_to_all | solution.py:373
  64.4 0.2 convert_reduce_fusion.lows
  64.6 16.0 %shard_map.106 = (bf16[16,64,256]{2,1,0:T(8,128)(2,1)S(1)}, f32[8,128]{1,0:T(8,128)S(1)}) custom-call(s32[16]{0:T(128)S(1)} %convert_reduce_fusion.lows, bf16[16,336,256]{2,1,0:T(8,128)(2,1)S(1)} %all-to-all-done.recv.qkv), custom_call_target="tpu_custom_call" | custom-call | flops 17179869184 | bytes 2097152 | tf_op jit(solution)/shard_map/pallas_call | solution.py:49
  80.6 0.0 copy-start.13
  80.6 0.6 copy-done.13
  81.2 0.0 all-to-all-done.1.recv.recv_hbm
  81.2 5.2 %shard_map.107 = (bf16[256,256]{1,0:T(8,128)(2,1)}, f32[16,64,256]{2,1,0:T(8,128)}, bf16[16,64,256]{2,1,0:T(8,128)(2,1)}) custom-call(s32[1]{0:T(128)} %bitcast.9.core, bf16[16,128,256]{2,1,0:T(8,128)(2,1)} %all-to-all-done.1.recv.recv_hbm, bf16[3,2048,256]{2,1,0:T(8,128)(2,1)} %copy-done.9, f32[256,256]{1,0:T(8,128)} %copy-done.11, f32[8,128]{1,0:T(8,128)} %copy-done.13), custom_call_target="tpu_custom_call" | custom-call | flops 2147483648 | bytes 6291456 | tf_op jit(solution)/shard_map/pallas_call | solution.py:49
  86.4 1.9 %collective-permute-start = (bf16[16,64,256]{2,1,0:T(8,128)(2,1)}, bf16[16,64,256]{2,1,0:T(8,128)(2,1)S(1)}, u32[]{:S(2)}, u32[]{:S(2)}) collective-permute-start(bf16[16,64,256]{2,1,0:T(8,128)(2,1)} %get-tuple-element.33), channel_id=1, source_target_pairs={{0,16},{16,0},{32,48},{48,32},{64,80},{80,64},{96,112},{112,96},{1... | collective-permute-start | bytes 1572872 | tf_op jit(solution)/shard_map/ppermute | solution.py:460
  88.3 1.7 %collective-permute-done = bf16[16,64,256]{2,1,0:T(8,128)(2,1)S(1)} collective-permute-done((bf16[16,64,256]{2,1,0:T(8,128)(2,1)}, bf16[16,64,256]{2,1,0:T(8,128)(2,1)S(1)}, u32[]{:S(2)}, u32[]{:S(2)}) %collective-permute-start) | collective-permute-done | bytes 524320 | tf_op jit(solution)/shard_map/ppermute | solution.py:460
  90.1 1.4 add_convert_fusion
  91.5 1.1 pad_maximum_fusion
  92.5 0.0 copy-start.7
  92.5 6.9 %all-to-all-start.2 = ((bf16[16,128,256]{2,1,0:T(8,128)(2,1)}), bf16[16,128,256]{2,1,0:T(8,128)(2,1)S(1)}, u32[]{:S(2)}, u32[]{:S(2)}) async-start(bf16[16,128,256]{2,1,0:T(8,128)(2,1)} %pad_maximum_fusion), calls=%async_computation.2 | async-start | bytes 2097152 | tf_op jit(solution)/shard_map/all_to_all | solution.py:373
  99.5 0.0 copy-done.7
  99.5 2.9 %shard_map.105 = (bf16[256,2048]{1,0:T(8,128)(2,1)}, f32[8,128]{1,0:T(8,128)S(1)}) custom-call(bf16[16,128,256]{2,1,0:T(8,128)(2,1)} %all-to-all-done.1.recv.recv_hbm, bf16[256,256]{1,0:T(8,128)(2,1)S(1)} %copy-done.8, bf16[256,32]{1,0:T(8,128)(2,1)S(1)} %copy-done.10, f32[256,2048]{1,0:T(8,128)S(1)} %copy-done.7), custom_call_target="tpu_custom_call" | custom-call | flops 1073741824 | bytes 4194304 | tf_op jit(solution)/shard_map/pallas_call | solution.py:49
  102.4 13.4 %all-to-all-done.2.recv = bf16[16,128,256]{2,1,0:T(8,128)(2,1)S(1)} async-done(((bf16[16,128,256]{2,1,0:T(8,128)(2,1)}), bf16[16,128,256]{2,1,0:T(8,128)(2,1)S(1)}, u32[]{:S(2)}, u32[]{:S(2)}) %all-to-all-start.2) | async-done | bytes 1048608 | tf_op jit(solution)/shard_map/all_to_all | solution.py:373
  115.8 0.8 shard_map.108
  116.6 9.8 %all-to-all-start.3 = ((bf16[8,64,256]{2,1,0:T(8,128)(2,1)}), bf16[8,64,256]{2,1,0:T(8,128)(2,1)S(1)}, u32[]{:S(2)}, u32[]{:S(2)}) async-start(bf16[8,64,256]{2,1,0:T(8,128)(2,1)} %shard_map.108), calls=%async_computation.3 | async-start | bytes 524288 | tf_op jit(solution)/shard_map/all_to_all | solution.py:373
  126.4 1.0 shard_map.109
  127.4 8.4 %all-to-all-done.3.recv = bf16[8,64,256]{2,1,0:T(8,128)(2,1)S(1)} async-done(((bf16[8,64,256]{2,1,0:T(8,128)(2,1)}), bf16[8,64,256]{2,1,0:T(8,128)(2,1)S(1)}, u32[]{:S(2)}, u32[]{:S(2)}) %all-to-all-start.3) | async-done | bytes 262176 | tf_op jit(solution)/shard_map/all_to_all | solution.py:373
  135.9 0.1 shard_map.110
  135.9 14.9 %all_to_all.25.mine = bf16[16,64,256]{2,1,0:T(8,128)(2,1)S(1)} all-to-all(bf16[16,64,256]{2,1,0:T(8,128)(2,1)S(1)} %shard_map.110), channel_id=1, replica_groups=mesh['dp'=16,'ctx'=16] {'ctx'}, dimensions={0} | all-to-all | bytes 1048576 | tf_op jit(solution)/shard_map/all_to_all | solution.py:373
  150.8 3.2 %collective-permute-start.1 = (bf16[16,64,256]{2,1,0:T(8,128)(2,1)S(1)}, bf16[16,64,256]{2,1,0:T(8,128)(2,1)S(1)}, u32[]{:S(2)}, u32[]{:S(2)}) collective-permute-start(bf16[16,64,256]{2,1,0:T(8,128)(2,1)S(1)} %all_to_all.25.mine), channel_id=1, source_target_pairs={{0,16},{16,0},{32,48},{48,32},{64,80},{80,64},{96,112},{112,96},{1... | collective-permute-start | bytes 1572872 | tf_op jit(solution)/shard_map/ppermute | solution.py:475
  154.0 1.5 collective-permute-done.1.other
  155.6 1.5 shard_map.111
  (2 shorter events, 0.0 us)
Async XLA Ops:
  8.4 7.8 %copy-start.4 = (bf16[1,256,32]{1,2,0:T(8,128)(2,1)S(1)}, bf16[1,256,32]{1,2,0:T(8,128)(2,1)}, u32[]{:S(2)}) copy-start(bf16[1,256,32]{1,2,0:T(8,128)(2,1)} %param.10) | copy-start | bytes 49156
  8.4 7.8 %copy-start.5 = (s32[1,256]{1,0:T(1,128)S(1)}, s32[1,256]{1,0:T(1,128)}, u32[]{:S(2)}) copy-start(s32[1,256]{1,0:T(1,128)} %ids.1) | copy-start | bytes 3076
  8.5 7.8 %copy-start.8 = (bf16[256,256]{1,0:T(8,128)(2,1)S(1)}, bf16[256,256]{1,0:T(8,128)(2,1)}, u32[]{:S(2)}) copy-start(bf16[256,256]{1,0:T(8,128)(2,1)} %get-tuple-element.22.proj) | copy-start | bytes 393220
  8.5 7.8 %copy-start.10 = (bf16[256,32]{1,0:T(8,128)(2,1)S(1)}, bf16[256,32]{1,0:T(8,128)(2,1)}, u32[]{:S(2)}) copy-start(bf16[256,32]{1,0:T(8,128)(2,1)} %get-tuple-element.23.te) | copy-start | bytes 49156
  8.5 7.8 %copy-start.12 = (bf16[256,32]{1,0:T(8,128)(2,1)S(1)}, bf16[256,32]{1,0:T(8,128)(2,1)}, u32[]{:S(2)}) copy-start(bf16[256,32]{1,0:T(8,128)(2,1)} %get-tuple-element.24.fs) | copy-start | bytes 49156
  8.5 48.5 %all-to-all-start = ((bf16[16,336,256]{2,1,0:T(8,128)(2,1)}), bf16[16,336,256]{2,1,0:T(8,128)(2,1)S(1)}, u32[]{:S(2)}, u32[]{:S(2)}) async-start(bf16[16,336,256]{2,1,0:T(8,128)(2,1)} %get-tuple-element.21), calls=%async_computation | async-start | bytes 5505024 | tf_op jit(solution)/shard_map/all_to_all | solution.py:373
  16.3 1.2 copy-start.1
  17.5 1.2 copy-start.2
  18.7 1.2 copy-start.3
  24.5 1.3 copy-start.6
  25.8 1.6 %copy-start.9 = (bf16[3,2048,256]{2,1,0:T(8,128)(2,1)}, bf16[3,2048,256]{2,1,0:T(8,128)(2,1)S(1)}, u32[]{:S(2)}) copy-start(bf16[3,2048,256]{2,1,0:T(8,128)(2,1)S(1)} %get-tuple-element.28.kept_hbm) | copy-start | bytes 9437188
  27.5 0.7 copy-start.11
  59.1 1.0 copy-start
  60.1 21.1 %all-to-all-start.1 = ((bf16[16,128,256]{2,1,0:T(8,128)(2,1)}), bf16[16,128,256]{2,1,0:T(8,128)(2,1)}, u32[]{:S(2)}, u32[]{:S(2)}) async-start(bf16[16,128,256]{2,1,0:T(8,128)(2,1)} %copy-done), calls=%async_computation.1 | async-start | bytes 2097152 | tf_op jit(solution)/shard_map/all_to_all | solution.py:373
  80.6 0.6 copy-start.13
  86.4 3.7 %collective-permute-start = (bf16[16,64,256]{2,1,0:T(8,128)(2,1)}, bf16[16,64,256]{2,1,0:T(8,128)(2,1)S(1)}, u32[]{:S(2)}, u32[]{:S(2)}) collective-permute-start(bf16[16,64,256]{2,1,0:T(8,128)(2,1)} %get-tuple-element.33), channel_id=1, source_target_pairs={{0,16},{16,0},{32,48},{48,32},{64,80},{80,64},{96,112},{112,96},{1... | collective-permute-start | bytes 1572872 | tf_op jit(solution)/shard_map/ppermute | solution.py:460
  92.5 7.0 %copy-start.7 = (f32[256,2048]{1,0:T(8,128)S(1)}, f32[256,2048]{1,0:T(8,128)}, u32[]{:S(2)}) copy-start(f32[256,2048]{1,0:T(8,128)} %copy-done.6) | copy-start | bytes 6291460
  92.5 23.3 %all-to-all-start.2 = ((bf16[16,128,256]{2,1,0:T(8,128)(2,1)}), bf16[16,128,256]{2,1,0:T(8,128)(2,1)S(1)}, u32[]{:S(2)}, u32[]{:S(2)}) async-start(bf16[16,128,256]{2,1,0:T(8,128)(2,1)} %pad_maximum_fusion), calls=%async_computation.2 | async-start | bytes 2097152 | tf_op jit(solution)/shard_map/all_to_all | solution.py:373
  116.6 19.3 %all-to-all-start.3 = ((bf16[8,64,256]{2,1,0:T(8,128)(2,1)}), bf16[8,64,256]{2,1,0:T(8,128)(2,1)S(1)}, u32[]{:S(2)}, u32[]{:S(2)}) async-start(bf16[8,64,256]{2,1,0:T(8,128)(2,1)} %shard_map.108), calls=%async_computation.3 | async-start | bytes 524288 | tf_op jit(solution)/shard_map/all_to_all | solution.py:373
  150.8 4.7 %collective-permute-start.1 = (bf16[16,64,256]{2,1,0:T(8,128)(2,1)S(1)}, bf16[16,64,256]{2,1,0:T(8,128)(2,1)S(1)}, u32[]{:S(2)}, u32[]{:S(2)}) collective-permute-start(bf16[16,64,256]{2,1,0:T(8,128)(2,1)S(1)} %all_to_all.25.mine), channel_id=1, source_target_pairs={{0,16},{16,0},{32,48},{48,32},{64,80},{80,64},{96,112},{112,96},{1... | collective-permute-start | bytes 1572872 | tf_op jit(solution)/shard_map/ppermute | solution.py:475

commit v3 on v2

--- a/solution.py
+++ b/solution.py
@@ -41,7 +41,7 @@
     return mm_nt(eye, jnp.broadcast_to(id_row, (128, n)).astype(bf16))
 
 
-def call(kernel, out_shape, *args, scratch=(), flops=0, n_bytes=4 << 20, prefetch=0, limit=24 << 20, hbm=(), out_hbm=False):
+def call(kernel, out_shape, *args, scratch=(), flops=0, n_bytes=4 << 20, prefetch=0, limit=24 << 20, hbm=()):
     vmem = pl.BlockSpec(memory_space=pltpu.VMEM)
     smem = pl.BlockSpec(memory_space=pltpu.SMEM)
     any_hbm = pl.BlockSpec(memory_space=pltpu.HBM)
@@ -50,7 +50,7 @@
         kernel,
         out_shape=out_shape,
         in_specs=[smem if k < prefetch else any_hbm if k in hbm else vmem for k in range(len(args))],
-        out_specs=[vmem] * len(out_shape) if many else any_hbm if out_hbm else vmem,
+        out_specs=[vmem] * len(out_shape) if many else vmem,
         scratch_shapes=list(scratch),
         compiler_params=pltpu.CompilerParams(vmem_limit_bytes=limit),
         cost_estimate=pl.CostEstimate(flops=flops, bytes_accessed=n_bytes, transcendentals=0),
@@ -118,6 +118,7 @@
     gains = jnp.concatenate(
         [jnp.broadcast_to(gain_hi.astype(f32), (8, heads)), jnp.broadcast_to(gain_lo.astype(f32), (8, heads))]
     ).astype(bf16)
+    all_gains = mm(gains, head_spread(heads, width, 0))
     row = iota((16, 256), 0)
     ends = jnp.where(row == 0, id_row, jnp.where(row == 3, id_row[:, :1], id_row[:, n_tok - 1 :]))
 
@@ -132,6 +133,8 @@
     proj_t = proj.astype(f32).T.astype(bf16)
     half = proj.shape[1] // 2
     b_t, c_t = proj_t[:half], proj_t[half:]
+    for m in range(3):
+        whole[2 + m].wait()
     sends = []
     for i in range(owners // 2):
         if i % 2 == 0:
@@ -143,7 +146,7 @@
         gs = (g[:, cols].astype(f32) * mm(from_start, spread)).astype(bf16)
         end_state = mm(b_t, xs).astype(bf16)
         start_grad = mm(c_t, gs).astype(bf16)
-        gain_rows = mm(gains, spread)
+        gain_rows = all_gains[:, cols]
         for k in range(2):
             part = slice(128 * k, 128 * k + 128)
             buf[2 * i + k, 0:128, 0:128] = end_state[:, part]
@@ -152,12 +155,6 @@
             gain_lo_row = jnp.concatenate([gain_rows[8:9, part]] * 2, axis=1)
             meta = jnp.where(row == 1, gain_hi_row, jnp.where(row == 2, gain_lo_row, ends))
             buf[2 * i + k, 128:144, :] = meta.astype(bf16)
-        span = (pl.ds(2 * i, 2), pl.ds(0, 144))
-        sends.append(pltpu.make_async_copy(buf.at[span], buf_hbm.at[span], out_sem.at[0, i]))
-        sends[-1].start()
-    for m in range(3):
-        whole[2 + m].wait()
-    for i in range(owners // 2):
         for m in range(3):
             block = qkv[m, :, 128 * i : 128 * i + 128].astype(f32)
             if m == 0:
@@ -166,14 +163,14 @@
             at = slice(144 + HEAD * m, 144 + HEAD * m + HEAD)
             buf[2 * i, at, :] = turned[:HEAD]
             buf[2 * i + 1, at, :] = turned[HEAD:]
-        span = (pl.ds(2 * i, 2), pl.ds(144, 192))
-        sends.append(pltpu.make_async_copy(buf.at[span], buf_hbm.at[span], out_sem.at[1, i]))
+        span = pl.ds(2 * i, 2)
+        sends.append(pltpu.make_async_copy(buf.at[span], buf_hbm.at[span], out_sem.at[i]))
         sends[-1].start()
     for copy in sends:
         copy.wait()
 
 
-def chain_kernel(recv, after, send_hbm, send, sem):
+def chain_kernel(recv, after, send):
     count = recv.shape[0]
     meta = [recv[k, 128:144, :].astype(f32) for k in range(count)]
     gain = [m[1:2, :128] + m[2:3, :128] for m in meta]
@@ -186,14 +183,9 @@
         send[k, :, 0:128] = state.astype(bf16)
         state = state * gain[k] + recv[k, 0:128, 0:128].astype(f32)
     adjoint = jnp.zeros((128, 128), f32)
-    copies = []
     for k in range(count - 1, -1, -1):
         send[k, :, 128:256] = adjoint.astype(bf16)
-        copies.append(pltpu.make_async_copy(send.at[k], send_hbm.at[k], sem.at[k]))
-        copies[-1].start()
         adjoint = (adjoint * gain[k] + recv[k, 0:128, 128:256].astype(f32)) * link[k]
-    for copy in copies:
-        copy.wait()
 
 
 def intra_kernel(inp, proj, x, g, te, fs, decay_t, ids, d_out, grad_out, kept, done, mixed):
@@ -269,9 +261,9 @@
     rows = kept.shape[1] // owners // 2
     mine = pl.multiple_of(core[0] * rows, rows)
     other = pl.multiple_of(rows - core[0] * rows, rows)
-    for j in range(owners):
-        keep[j] = mm(kept[2, pl.ds(2 * rows * j + mine, rows), :], og)
-        give[j] = mm(kept[2, pl.ds(2 * rows * j + other, rows), :], og).astype(bf16)
+    for first, out in ((mine, keep), (other, give)):
+        half = jnp.concatenate([kept[2, pl.ds(2 * rows * j + first, rows), :] for j in range(owners)])
+        out[...] = mm(half, og).astype(bf16).reshape(out.shape)
 
 
 def input_grad_kernel(recv, proj, te, d_in, dx_out, done):
@@ -349,16 +341,19 @@
 def unpack_kernel(recv, out, done):
     done[...] = jnp.zeros(done.shape, f32)
     for i in range(recv.shape[0] // 2):
-        tall = jnp.concatenate([recv[2 * i, 64:128], recv[2 * i + 1, 64:128]]).astype(f32)
+        tall = jnp.concatenate([recv[2 * i], recv[2 * i + 1]]).astype(f32)
         out[:, 128 * i : 128 * i + 128] = tall.T.astype(bf16)
 
 
-def sum_kernel(recv, after, out):
-    rows = out.shape[1]
-    total = recv[0, 0:rows, :].astype(f32)
+def share_sum_kernel(recv, after, passed, out, passed_out):
+    total = recv[0].astype(f32)
     for k in range(1, recv.shape[0]):
-        total += recv[k, 0:rows, :].astype(f32)
-    total = total.astype(bf16)
+        total += recv[k].astype(f32)
+    out[...] = total.astype(bf16)
+
+
+def plane_sum_kernel(part, met, after, out):
+    total = (part[...].astype(f32) + met[...].astype(f32)).astype(bf16)
     for k in range(out.shape[0]):
         out[k] = total
 
@@ -369,8 +364,8 @@
         out[j, 1 - core[0]] = other[j].astype(f32) * scale
 
 
-def exchange(blocks, axis, groups=None):
-    return lax.all_to_all(blocks, axis, split_axis=0, concat_axis=0, tiled=True, axis_index_groups=groups)
+def exchange(blocks, axis):
+    return lax.all_to_all(blocks, axis, split_axis=0, concat_axis=0, tiled=True)
 
 
 def per_device(layer_input, proj_weight, ssd_input, log_decay, segment_ids, ssd_cotangent, window_qkv):
@@ -384,7 +379,6 @@
     n_out = proj_weight.shape[1]
     core = lax.axis_index("dp") % 2
     pairs = [(i, i ^ 1) for i in range(dp)]
-    planes = [list(range(c, dp, 2)) for c in range(2)]
 
     done = sds((8, 128), f32)
 
@@ -407,7 +401,7 @@
             pltpu.VMEM((ctx, 336, n_tok), bf16),
             pltpu.SemaphoreType.DMA((13,)),
             pltpu.SemaphoreType.DMA((2, 4)),
-            pltpu.SemaphoreType.DMA((2, ctx // 2)),
+            pltpu.SemaphoreType.DMA((ctx // 2,)),
         ],
         compiler_params=pltpu.CompilerParams(vmem_limit_bytes=64 << 20),
         cost_estimate=pl.CostEstimate(flops=2 << 30, bytes_accessed=9 << 20, transcendentals=0),
@@ -430,8 +424,7 @@
         chain_kernel,
         sds((ctx, 128, 256), bf16),
         got, intra_done,
-        scratch=[pltpu.VMEM((ctx, 128, 256), bf16), pltpu.SemaphoreType.DMA((ctx,))],
-        n_bytes=6 << 20, limit=24 << 20, out_hbm=True,
+        n_bytes=6 << 20,
     )
     back = exchange(sent, "ctx")
 
@@ -448,29 +441,44 @@
     half_rows = width // ctx // 2
     out_grad, keep, give = call(
         outer_kernel,
-        (sds((n_tok, n_out), bf16), sds((ctx, half_rows, n_out), f32), sds((ctx, half_rows, n_out), bf16)),
+        (sds((n_tok, n_out), bf16), sds((ctx, half_rows, n_out), bf16), sds((ctx, half_rows, n_out), bf16)),
         core[None], back, kept, grad_intra, attention_done,
         scratch=[
             pltpu.VMEM((ctx, 128, 256), bf16),
             pltpu.VMEM((3, width, n_tok), bf16),
             pltpu.SemaphoreType.DMA((13,)),
         ],
-        flops=2 << 30, n_bytes=6 << 20, prefetch=1, limit=62 << 20, hbm=(1, 2),
-    )
-    share = (keep + lax.ppermute(give, "dp", pairs).astype(f32)).astype(bf16)
-    third = exchange(jnp.concatenate([share, attended], axis=1), "ctx")
+        flops=2 << 30, n_bytes=6 << 20, prefetch=1, limit=61 << 20, hbm=(1, 2),
+    )
+    given = lax.ppermute(give, "dp", pairs)
+    share = (keep.astype(f32) + given.astype(f32)).astype(bf16)
+    shares = exchange(share, "ctx")
     input_grad, input_done = call(
         input_grad_kernel,
         (sds((n_tok, width), bf16), done),
         back, proj, te, d_intra,
         flops=1 << 30, n_bytes=4 << 20,
     )
-    part = call(sum_kernel, sds((dp // 2, half_rows, n_out), bf16), third, input_done, n_bytes=2 << 20)
-    parts = exchange(part, "dp", planes)
+    part, attended = pl.pallas_call(
+        share_sum_kernel,
+        out_shape=(sds((half_rows, n_out), bf16), sds(attended.shape, bf16)),
+        in_specs=[vmem, vmem, anywhere],
+        out_specs=(vmem, anywhere),
+        input_output_aliases={2: 1},
+        compiler_params=pltpu.CompilerParams(vmem_limit_bytes=24 << 20),
+        cost_estimate=pl.CostEstimate(flops=0, bytes_accessed=1 << 20, transcendentals=0),
+    )(shares, input_done, attended)
+    out_rows = exchange(attended, "ctx")
     window_out, window_done = call(
-        unpack_kernel, (sds((n_tok, ctx * HEAD), bf16), done), third, n_bytes=1 << 20
-    )
-    strip = call(sum_kernel, sds((ctx, half_rows, n_out), bf16), parts, window_done, n_bytes=1 << 20)
+        unpack_kernel, (sds((n_tok, ctx * HEAD), bf16), done), out_rows, n_bytes=1 << 20
+    )
+    step = 2
+    while 2 * step < dp:
+        met = lax.ppermute(part, "dp", [(i, i ^ step) for i in range(dp)])
+        part = (part.astype(f32) + met.astype(f32)).astype(bf16)
+        step *= 2
+    met = lax.ppermute(part, "dp", [(i, i ^ step) for i in range(dp)])
+    strip = call(plane_sum_kernel, sds((ctx, half_rows, n_out), bf16), part, met, window_done, n_bytes=1 << 20)
     mine = exchange(strip, "ctx")
     other = lax.ppermute(mine, "dp", pairs)
     weight_grad = call(

time: 157 us -> 152 us (0.968)
  waiting for transfers between devices: 53.9 us -> 41.7 us
  starting transfers between devices: 34 us -> 43.5 us
  Pallas kernels: 41.6 us -> 39 us
    all_to_all x4, waiting for transfers between devices: 50.7 us -> 36.7 us  [exchange(): return lax.all_to_all(blocks, axis, split_axis=0, concat_axis=0, tiled=True)]
    ppermute x1 -> x4, starting transfers between devices: 1.92 us -> 15 us  [the longest x3 13.7 us: per_device(): met = lax.ppermute(part, 'dp', [(i, i ^ step) for i in range(dp)])]
    all_to_all x4, starting transfers between devices: 28.9 us -> 22.5 us  [exchange(): return lax.all_to_all(blocks, axis, split_axis=0, concat_axis=0, tiled=True)]
    ppermute x1, starting transfers between devices: 3.18 us -> 6.06 us  [per_device(): other = lax.ppermute(mine, 'dp', pairs)]
    pallas_call x9 -> x8, Pallas kernels: 33.8 us -> 31.8 us  [call(): pl.pallas_call(kernel, out_shape=out_shape, in_specs=[smem if k < prefetc...]
    ppermute x1 -> x4, waiting for transfers between devices: 1.75 us -> 3.51 us  [the longest x3 1.76 us: per_device(): met = lax.ppermute(part, 'dp', [(i, i ^ step) for i in range(dp)])]
  transfers between devices with their start and end apart: 6 -> 9, of which waited for: 5 -> 6; matrix products, arithmetic and copies ran while one was open for 0% -> 0% of each run, Pallas kernels for 16% -> 17%
where the time goes in v3:
time: 152 us
  starting transfers between devices  43.5 us (29%)
  waiting for transfers between devices  41.7 us (27%)
  Pallas kernels  39 us (26%)
  blocking collectives  15.7 us (10%)
  local copies, waits for them, and re-layouts  9.09 us (6%)
  other arithmetic  2.22 us (1%)
    all_to_all x4, waiting for transfers between devices, exchange(): return lax.all_to_all(blocks, axis, split_axis=0, concat_axis=0, tiled=True)  36.7 us
    pallas_call x8, Pallas kernels, call(): pl.pallas_call(kernel, out_shape=out_shape, in_specs=[smem if k < prefetc...  31.8 us
    all_to_all x4, starting transfers between devices, exchange(): return lax.all_to_all(blocks, axis, split_axis=0, concat_axis=0, tiled=True)  22.5 us
    all_to_all x1, blocking collectives, exchange(): return lax.all_to_all(blocks, axis, split_axis=0, concat_axis=0, tiled=True)  15.7 us
    ppermute x3, starting transfers between devices, per_device(): met = lax.ppermute(part, 'dp', [(i, i ^ step) for i in range(dp)])  13.7 us
    unnamed x29, local copies, waits for them, and re-layouts  8.91 us
    pallas_call x1, Pallas kernels, per_device(): pl.pallas_call(front_kernel, out_shape=(sds((ctx, 336, n_tok), bf16), sds...  7.12 us
    ppermute x1, starting transfers between devices, per_device(): other = lax.ppermute(mine, 'dp', pairs)  6.06 us
  transfers between devices with their start and end apart: 9, of which 6 were waited for; matrix products, arithmetic and copies ran while one was open for 0% of the time, Pallas kernels for 17%

profile of v3, /device:TPU:1, one launch (start us, length us, event | category | flops | bytes accessed | tf_op | source)
XLA Modules:
  0.0 152.1 jit_solution(7505751562465022470)
XLA Ops:
  0.6 7.1 %shard_map.102 = (bf16[16,336,256]{2,1,0:T(8,128)(2,1)}, bf16[256,256]{1,0:T(8,128)(2,1)}, bf16[256,32]{1,0:T(8,128)(2,1)}, bf16[256,32]{1,0:T(8,128)(2,1)}) custom-call(bf16[256,2048]{1,0:T(8,128)(2,1)} %bitcast.17, bf16[2048,256]{1,0:T(8,128)(2,1)} %w_hbm.1, bf16[256,2048]{1,0:T(8,128)(2,1)} %bitcast.19, bf16[256,2048]{1,0:T(8,128)(2,1)} %bitcast.21, ...), custom_call_target="tpu_custom_call" | custom-call | flops 2147483648 | bytes 9437184 | tf_op jit(solution)/shard_map/pallas_call | solution.py:387
  7.8 0.0 copy-start.4
  7.8 0.0 copy-start.5
  7.8 0.0 copy-start.8
  7.8 0.0 copy-start.10
  7.8 0.0 copy-start.12
  7.8 7.7 %all-to-all-start = ((bf16[16,336,256]{2,1,0:T(8,128)(2,1)}), bf16[16,336,256]{2,1,0:T(8,128)(2,1)S(1)}, u32[]{:S(2)}, u32[]{:S(2)}) async-start(bf16[16,336,256]{2,1,0:T(8,128)(2,1)} %get-tuple-element.23), calls=%async_computation | async-start | bytes 5505024 | tf_op jit(solution)/shard_map/all_to_all | solution.py:368
  15.6 0.0 copy-done.4
  15.6 0.0 copy-done.5
  15.6 0.0 copy-done.8
  15.6 0.0 copy-done.10
  15.6 0.0 copy-done.12
  15.6 0.0 copy-start.1
  15.6 1.2 copy-done.1
  16.8 0.0 copy-start.2
  16.9 1.2 copy-done.2
  18.1 0.0 copy-start.3
  18.1 1.2 copy-done.3
  19.3 4.5 %shard_map.103 = (f32[256,2048]{1,0:T(8,128)S(1)}, f32[256,256]{1,0:T(8,128)S(1)}, bf16[3,2048,256]{2,1,0:T(8,128)(2,1)S(1)}, f32[8,128]{1,0:T(8,128)S(1)}) custom-call(bf16[256,2048]{1,0:T(8,128)(2,1)S(1)} %bitcast.18, bf16[256,256]{1,0:T(8,128)(2,1)S(1)} %copy-done.8, bf16[256,2048]{1,0:T(8,128)(2,1)S(1)} %bitcast.20, bf16[256,2048]{1,0:T(8,128)(2,1)S(1)} %bitcast.22, ...), custom_call_target="tpu_custom_call" | custom-call | flops 6442450944 | bytes 8388608 | tf_op jit(solution)/shard_map/pallas_call | solution.py:49
  23.8 0.0 copy-start.6
  23.8 1.3 copy-done.6
  25.1 0.0 copy-start.9
  25.1 1.6 %copy-done.9 = bf16[3,2048,256]{2,1,0:T(8,128)(2,1)} copy-done((bf16[3,2048,256]{2,1,0:T(8,128)(2,1)}, bf16[3,2048,256]{2,1,0:T(8,128)(2,1)S(1)}, u32[]{:S(2)}) %copy-start.9) | copy-done | bytes 3145752
  26.8 0.0 copy-start.11
  26.8 0.7 copy-done.11
  27.5 28.9 %all-to-all-done.recv.qkv = bf16[16,336,256]{2,1,0:T(8,128)(2,1)S(1)} async-done(((bf16[16,336,256]{2,1,0:T(8,128)(2,1)}), bf16[16,336,256]{2,1,0:T(8,128)(2,1)S(1)}, u32[]{:S(2)}, u32[]{:S(2)}) %all-to-all-start) | async-done | bytes 2752544 | tf_op jit(solution)/shard_map/all_to_all | solution.py:368
  56.4 0.2 slice_reduce_fusion
  56.6 0.3 shard_map.104
  56.9 0.0 copy-start
  56.9 1.0 copy-done
  57.9 4.3 %all-to-all-start.1 = ((bf16[16,128,256]{2,1,0:T(8,128)(2,1)}), bf16[16,128,256]{2,1,0:T(8,128)(2,1)}, u32[]{:S(2)}, u32[]{:S(2)}) async-start(bf16[16,128,256]{2,1,0:T(8,128)(2,1)} %copy-done), calls=%async_computation.1 | async-start | bytes 2097152 | tf_op jit(solution)/shard_map/all_to_all | solution.py:368
  62.2 0.2 convert_reduce_fusion.lows
  62.4 16.8 %shard_map.106 = (bf16[16,64,256]{2,1,0:T(8,128)(2,1)}, f32[8,128]{1,0:T(8,128)S(1)}) custom-call(s32[16]{0:T(128)S(1)} %convert_reduce_fusion.lows, bf16[16,336,256]{2,1,0:T(8,128)(2,1)S(1)} %all-to-all-done.recv.qkv), custom_call_target="tpu_custom_call" | custom-call | flops 17179869184 | bytes 2097152 | tf_op jit(solution)/shard_map/pallas_call | solution.py:49
  79.2 0.0 copy-start.13
  79.2 0.6 copy-done.13
  79.8 0.0 all-to-all-done.1.recv.recv_hbm
  79.8 0.0 copy-start.7
  79.8 4.8 %shard_map.107 = (bf16[256,256]{1,0:T(8,128)(2,1)}, bf16[16,64,256]{2,1,0:T(8,128)(2,1)}, bf16[16,64,256]{2,1,0:T(8,128)(2,1)}) custom-call(s32[1]{0:T(128)} %bitcast.9.core, bf16[16,128,256]{2,1,0:T(8,128)(2,1)} %all-to-all-done.1.recv.recv_hbm, bf16[3,2048,256]{2,1,0:T(8,128)(2,1)} %copy-done.9, f32[256,256]{1,0:T(8,128)} %copy-done.11, f32[8,128]{1,0:T(8,128)} %copy-done.13), custom_call_target="tpu_custom_call" | custom-call | flops 2147483648 | bytes 6291456 | tf_op jit(solution)/shard_map/pallas_call | solution.py:49
  84.6 1.3 collective-permute-start
  85.9 1.7 %collective-permute-done = bf16[16,64,256]{2,1,0:T(8,128)(2,1)S(1)} collective-permute-done((bf16[16,64,256]{2,1,0:T(8,128)(2,1)}, bf16[16,64,256]{2,1,0:T(8,128)(2,1)S(1)}, u32[]{:S(2)}, u32[]{:S(2)}) %collective-permute-start) | collective-permute-done | bytes 524320 | tf_op jit(solution)/shard_map/ppermute | solution.py:453
  87.6 2.0 %add_convert_fusion = bf16[16,64,256]{2,1,0:T(8,128)(2,1)} fusion(bf16[16,64,256]{2,1,0:T(8,128)(2,1)S(1)} %collective-permute-done, bf16[16,64,256]{2,1,0:T(8,128)(2,1)} %get-tuple-element.34), kind=kLoop, calls=%fused_computation | loop fusion | flops 1048576 | bytes 1572864 | tf_op jit(solution)/shard_map/convert_element_type | solution.py:454
  89.6 6.8 %all-to-all-start.2 = ((bf16[16,64,256]{2,1,0:T(8,128)(2,1)}), bf16[16,64,256]{2,1,0:T(8,128)(2,1)S(1)}, u32[]{:S(2)}, u32[]{:S(2)}) async-start(bf16[16,64,256]{2,1,0:T(8,128)(2,1)} %add_convert_fusion), calls=%async_computation.2 | async-start | bytes 1048576 | tf_op jit(solution)/shard_map/all_to_all | solution.py:368
  96.4 0.0 copy-done.7
  96.4 2.9 %shard_map.105 = (bf16[256,2048]{1,0:T(8,128)(2,1)}, f32[8,128]{1,0:T(8,128)S(1)}) custom-call(bf16[16,128,256]{2,1,0:T(8,128)(2,1)} %all-to-all-done.1.recv.recv_hbm, bf16[256,256]{1,0:T(8,128)(2,1)S(1)} %copy-done.8, bf16[256,32]{1,0:T(8,128)(2,1)S(1)} %copy-done.10, f32[256,2048]{1,0:T(8,128)S(1)} %copy-done.7), custom_call_target="tpu_custom_call" | custom-call | flops 1073741824 | bytes 4194304 | tf_op jit(solution)/shard_map/pallas_call | solution.py:49
  99.3 7.8 %all-to-all-done.2.recv = bf16[16,64,256]{2,1,0:T(8,128)(2,1)S(1)} async-done(((bf16[16,64,256]{2,1,0:T(8,128)(2,1)}), bf16[16,64,256]{2,1,0:T(8,128)(2,1)S(1)}, u32[]{:S(2)}, u32[]{:S(2)}) %all-to-all-start.2) | async-done | bytes 524320 | tf_op jit(solution)/shard_map/all_to_all | solution.py:368
  107.1 0.1 shard_map.108
  107.2 3.4 %collective-permute-start.1 = (bf16[64,256]{1,0:T(8,128)(2,1)S(1)}, bf16[64,256]{1,0:T(8,128)(2,1)S(1)}, u32[]{:S(2)}, u32[]{:S(2)}) collective-permute-start(bf16[64,256]{1,0:T(8,128)(2,1)S(1)} %get-tuple-element.38), channel_id=1, source_target_pairs={{0,32},{16,48},{32,0},{48,16},{64,96},{80,112},{96,64},{112,80},{1... | collective-permute-start | bytes 98312 | tf_op jit(solution)/shard_map/ppermute | solution.py:477
  110.6 3.6 %all-to-all-start.3 = ((bf16[16,64,256]{2,1,0:T(8,128)(2,1)}), bf16[16,64,256]{2,1,0:T(8,128)(2,1)S(1)}, u32[]{:S(2)}, u32[]{:S(2)}) async-start(bf16[16,64,256]{2,1,0:T(8,128)(2,1)} %get-tuple-element.39), calls=%async_computation.3 | async-start | bytes 1048576 | tf_op jit(solution)/shard_map/all_to_all | solution.py:368
  114.2 0.0 collective-permute-done.1
  114.3 3.2 %collective-permute-start.2 = (bf16[64,256]{1,0:T(8,128)(2,1)S(1)}, bf16[64,256]{1,0:T(8,128)(2,1)S(1)}, u32[]{:S(2)}, u32[]{:S(2)}) collective-permute-start(bf16[64,256]{1,0:T(8,128)(2,1)S(1)} %add_convert_fusion.2), channel_id=1, source_target_pairs={{0,64},{16,80},{32,96},{48,112},{64,0},{80,16},{96,32},{112,48},{1... | collective-permute-start | bytes 98312 | tf_op jit(solution)/shard_map/ppermute | solution.py:477
  117.4 1.3 collective-permute-done.2
  118.8 7.1 %collective-permute-start.3 = (bf16[64,256]{1,0:T(8,128)(2,1)S(1)}, bf16[64,256]{1,0:T(8,128)(2,1)S(1)}, u32[]{:S(2)}, u32[]{:S(2)}) collective-permute-start(bf16[64,256]{1,0:T(8,128)(2,1)S(1)} %add_convert_fusion.1.part), channel_id=1, source_target_pairs={{0,128},{16,144},{32,160},{48,176},{64,192},{80,208},{96,224},{112... | collective-permute-start | bytes 98312 | tf_op jit(solution)/shard_map/ppermute | solution.py:480
  125.8 0.0 all-to-all-done.3.recv
  125.8 1.0 shard_map.109
  126.8 0.5 collective-permute-done.3.met
  127.4 15.7 %all_to_all.25.mine = bf16[16,64,256]{2,1,0:T(8,128)(2,1)S(1)} all-to-all(bf16[16,64,256]{2,1,0:T(8,128)(2,1)S(1)} %shard_map.110), channel_id=1, replica_groups=mesh['dp'=16,'ctx'=16] {'ctx'}, dimensions={0} | all-to-all | bytes 1048576 | tf_op jit(solution)/shard_map/all_to_all | solution.py:368
  143.0 6.1 %collective-permute-start.4 = (bf16[16,64,256]{2,1,0:T(8,128)(2,1)S(1)}, bf16[16,64,256]{2,1,0:T(8,128)(2,1)S(1)}, u32[]{:S(2)}, u32[]{:S(2)}) collective-permute-start(bf16[16,64,256]{2,1,0:T(8,128)(2,1)S(1)} %all_to_all.25.mine), channel_id=1, source_target_pairs={{0,16},{16,0},{32,48},{48,32},{64,80},{80,64},{96,112},{112,96},{1... | collective-permute-start | bytes 1572872 | tf_op jit(solution)/shard_map/ppermute | solution.py:483
  149.1 1.5 %collective-permute-done.4.other = bf16[16,64,256]{2,1,0:T(8,128)(2,1)S(1)} collective-permute-done((bf16[16,64,256]{2,1,0:T(8,128)(2,1)S(1)}, bf16[16,64,256]{2,1,0:T(8,128)(2,1)S(1)}, u32[]{:S(2)}, u32[]{:S(2)}) %collective-permute-start.4) | collective-permute-done | bytes 524320 | tf_op jit(solution)/shard_map/ppermute | solution.py:483
  150.6 1.5 shard_map.111
  (5 shorter events, 0.1 us)
Async XLA Ops:
  7.8 7.8 %copy-start.4 = (bf16[1,256,32]{1,2,0:T(8,128)(2,1)S(1)}, bf16[1,256,32]{1,2,0:T(8,128)(2,1)}, u32[]{:S(2)}) copy-start(bf16[1,256,32]{1,2,0:T(8,128)(2,1)} %param.10) | copy-start | bytes 49156
  7.8 7.8 %copy-start.5 = (s32[1,256]{1,0:T(1,128)S(1)}, s32[1,256]{1,0:T(1,128)}, u32[]{:S(2)}) copy-start(s32[1,256]{1,0:T(1,128)} %ids.1) | copy-start | bytes 3076
  7.8 7.8 %copy-start.8 = (bf16[256,256]{1,0:T(8,128)(2,1)S(1)}, bf16[256,256]{1,0:T(8,128)(2,1)}, u32[]{:S(2)}) copy-start(bf16[256,256]{1,0:T(8,128)(2,1)} %get-tuple-element.24.proj) | copy-start | bytes 393220
  7.8 7.8 %copy-start.10 = (bf16[256,32]{1,0:T(8,128)(2,1)S(1)}, bf16[256,32]{1,0:T(8,128)(2,1)}, u32[]{:S(2)}) copy-start(bf16[256,32]{1,0:T(8,128)(2,1)} %get-tuple-element.25.te) | copy-start | bytes 49156
  7.8 7.8 %copy-start.12 = (bf16[256,32]{1,0:T(8,128)(2,1)S(1)}, bf16[256,32]{1,0:T(8,128)(2,1)}, u32[]{:S(2)}) copy-start(bf16[256,32]{1,0:T(8,128)(2,1)} %get-tuple-element.26.fs) | copy-start | bytes 49156
  7.8 48.5 %all-to-all-start = ((bf16[16,336,256]{2,1,0:T(8,128)(2,1)}), bf16[16,336,256]{2,1,0:T(8,128)(2,1)S(1)}, u32[]{:S(2)}, u32[]{:S(2)}) async-start(bf16[16,336,256]{2,1,0:T(8,128)(2,1)} %get-tuple-element.23), calls=%async_computation | async-start | bytes 5505024 | tf_op jit(solution)/shard_map/all_to_all | solution.py:368
  15.6 1.2 copy-start.1
  16.8 1.2 copy-start.2
  18.1 1.2 copy-start.3
  23.8 1.3 copy-start.6
  25.1 1.6 %copy-start.9 = (bf16[3,2048,256]{2,1,0:T(8,128)(2,1)}, bf16[3,2048,256]{2,1,0:T(8,128)(2,1)S(1)}, u32[]{:S(2)}) copy-start(bf16[3,2048,256]{2,1,0:T(8,128)(2,1)S(1)} %get-tuple-element.30.kept_hbm) | copy-start | bytes 9437188
  26.8 0.7 copy-start.11
  56.9 1.0 copy-start
  57.9 21.9 %all-to-all-start.1 = ((bf16[16,128,256]{2,1,0:T(8,128)(2,1)}), bf16[16,128,256]{2,1,0:T(8,128)(2,1)}, u32[]{:S(2)}, u32[]{:S(2)}) async-start(bf16[16,128,256]{2,1,0:T(8,128)(2,1)} %copy-done), calls=%async_computation.1 | async-start | bytes 2097152 | tf_op jit(solution)/shard_map/all_to_all | solution.py:368
  79.2 0.6 copy-start.13
  79.8 16.7 %copy-start.7 = (f32[256,2048]{1,0:T(8,128)S(1)}, f32[256,2048]{1,0:T(8,128)}, u32[]{:S(2)}) copy-start(f32[256,2048]{1,0:T(8,128)} %copy-done.6) | copy-start | bytes 6291460
  84.6 3.0 %collective-permute-start = (bf16[16,64,256]{2,1,0:T(8,128)(2,1)}, bf16[16,64,256]{2,1,0:T(8,128)(2,1)S(1)}, u32[]{:S(2)}, u32[]{:S(2)}) collective-permute-start(bf16[16,64,256]{2,1,0:T(8,128)(2,1)} %get-tuple-element.35), channel_id=1, source_target_pairs={{0,16},{16,0},{32,48},{48,32},{64,80},{80,64},{96,112},{112,96},{1... | collective-permute-start | bytes 1572872 | tf_op jit(solution)/shard_map/ppermute | solution.py:453
  89.6 17.5 %all-to-all-start.2 = ((bf16[16,64,256]{2,1,0:T(8,128)(2,1)}), bf16[16,64,256]{2,1,0:T(8,128)(2,1)S(1)}, u32[]{:S(2)}, u32[]{:S(2)}) async-start(bf16[16,64,256]{2,1,0:T(8,128)(2,1)} %add_convert_fusion), calls=%async_computation.2 | async-start | bytes 1048576 | tf_op jit(solution)/shard_map/all_to_all | solution.py:368
  107.2 7.0 %collective-permute-start.1 = (bf16[64,256]{1,0:T(8,128)(2,1)S(1)}, bf16[64,256]{1,0:T(8,128)(2,1)S(1)}, u32[]{:S(2)}, u32[]{:S(2)}) collective-permute-start(bf16[64,256]{1,0:T(8,128)(2,1)S(1)} %get-tuple-element.38), channel_id=1, source_target_pairs={{0,32},{16,48},{32,0},{48,16},{64,96},{80,112},{96,64},{112,80},{1... | collective-permute-start | bytes 98312 | tf_op jit(solution)/shard_map/ppermute | solution.py:477
  110.6 15.2 %all-to-all-start.3 = ((bf16[16,64,256]{2,1,0:T(8,128)(2,1)}), bf16[16,64,256]{2,1,0:T(8,128)(2,1)S(1)}, u32[]{:S(2)}, u32[]{:S(2)}) async-start(bf16[16,64,256]{2,1,0:T(8,128)(2,1)} %get-tuple-element.39), calls=%async_computation.3 | async-start | bytes 1048576 | tf_op jit(solution)/shard_map/all_to_all | solution.py:368
  114.3 4.5 %collective-permute-start.2 = (bf16[64,256]{1,0:T(8,128)(2,1)S(1)}, bf16[64,256]{1,0:T(8,128)(2,1)S(1)}, u32[]{:S(2)}, u32[]{:S(2)}) collective-permute-start(bf16[64,256]{1,0:T(8,128)(2,1)S(1)} %add_convert_fusion.2), channel_id=1, source_target_pairs={{0,64},{16,80},{32,96},{48,112},{64,0},{80,16},{96,32},{112,48},{1... | collective-permute-start | bytes 98312 | tf_op jit(solution)/shard_map/ppermute | solution.py:477
  118.8 8.5 %collective-permute-start.3 = (bf16[64,256]{1,0:T(8,128)(2,1)S(1)}, bf16[64,256]{1,0:T(8,128)(2,1)S(1)}, u32[]{:S(2)}, u32[]{:S(2)}) collective-permute-start(bf16[64,256]{1,0:T(8,128)(2,1)S(1)} %add_convert_fusion.1.part), channel_id=1, source_target_pairs={{0,128},{16,144},{32,160},{48,176},{64,192},{80,208},{96,224},{112... | collective-permute-start | bytes 98312 | tf_op jit(solution)/shard_map/ppermute | solution.py:480
  143.0 7.6 %collective-permute-start.4 = (bf16[16,64,256]{2,1,0:T(8,128)(2,1)S(1)}, bf16[16,64,256]{2,1,0:T(8,128)(2,1)S(1)}, u32[]{:S(2)}, u32[]{:S(2)}) collective-permute-start(bf16[16,64,256]{2,1,0:T(8,128)(2,1)S(1)} %all_to_all.25.mine), channel_id=1, source_target_pairs={{0,16},{16,0},{32,48},{48,32},{64,80},{80,64},{96,112},{112,96},{1... | collective-permute-start | bytes 1572872 | tf_op jit(solution)/shard_map/ppermute | solution.py:483

commit v4 on v3

--- a/solution.py
+++ b/solution.py
@@ -266,7 +266,7 @@
         out[...] = mm(half, og).astype(bf16).reshape(out.shape)
 
 
-def input_grad_kernel(recv, proj, te, d_in, dx_out, done):
+def input_grad_kernel(recv, proj, te, d_in, after, dx_out, done):
     done[...] = jnp.zeros(done.shape, f32)
     owners = recv.shape[0]
     heads = te.shape[1]
@@ -278,9 +278,9 @@
         dx_out[:, cols] = (d_in[:, cols] + spread * mm(b_rows, leave)).astype(bf16)
 
 
-def attention_kernel(lows, qkv, out, done, keys, values):
+def attention_kernel(lows, qkv, after, out, done, keys, values, *, begin):
     done[...] = jnp.zeros(done.shape, f32)
-    blocks = qkv.shape[0]
+    blocks = begin + out.shape[0]
     n = qkv.shape[2]
     slot = iota((16, n), 0).astype(f32)
     zeros48 = jnp.zeros((48, n), f32)
@@ -294,7 +294,7 @@
         values[k, 64:80, :] = jnp.ones((16, n), bf16)
         return carry
 
-    lax.fori_loop(0, blocks, prepare, 0)
+    lax.fori_loop(lows[begin] // 2 * 2, blocks, prepare, 0)
     later = iota((2 * n, n), 0) - iota((2 * n, n), 1)
     masks = [jnp.where(later > k * n, -BIG, 0.0) for k in range(2)]
 
@@ -332,10 +332,10 @@
         held = lax.fori_loop(1, c + 1 - lows[2 * c] // 2, step, tuple(held))
         for k in range(2):
             total = held[2 * k + 1]
-            out[2 * c + k] = (total[0:64] / total[64:65]).astype(bf16)
+            out[2 * c + k - begin] = (total[0:64] / total[64:65]).astype(bf16)
         return carry
 
-    lax.fori_loop(0, blocks // 2, per_pair, 0)
+    lax.fori_loop(begin // 2, blocks // 2, per_pair, 0)
 
 
 def unpack_kernel(recv, out, done):
@@ -430,13 +430,17 @@
 
     ids = got[:, 128, :].astype(jnp.int32)
     lows = jnp.sum(ids[None, :, -1] < ids[:, None, 0], axis=1, dtype=jnp.int32)
-    attended, attention_done = call(
-        attention_kernel,
-        (sds((ctx, HEAD, n_tok), bf16), done),
-        lows, got,
-        scratch=[pltpu.VMEM((ctx * n_tok, 128), bf16), pltpu.VMEM((ctx, 80, n_tok), bf16)],
-        flops=16 << 30, n_bytes=2 << 20, prefetch=1,
-    )
+    def attend(begin, end, after):
+        return call(
+            functools.partial(attention_kernel, begin=begin),
+            (sds((end - begin, HEAD, n_tok), bf16), done),
+            lows, got, after,
+            scratch=[pltpu.VMEM((end * n_tok, 128), bf16), pltpu.VMEM((end, 80, n_tok), bf16)],
+            flops=8 << 30, n_bytes=2 << 20, prefetch=1, hbm=(2,),
+        )
+
+    split = ctx * 5 // 16 * 2
+    attended, attention_done = attend(0, split, lows)
 
     half_rows = width // ctx // 2
     out_grad, keep, give = call(
@@ -453,11 +457,12 @@
     given = lax.ppermute(give, "dp", pairs)
     share = (keep.astype(f32) + given.astype(f32)).astype(bf16)
     shares = exchange(share, "ctx")
+    attended = jnp.concatenate([attended, attend(split, ctx, share)[0]])
     input_grad, input_done = call(
         input_grad_kernel,
         (sds((n_tok, width), bf16), done),
-        back, proj, te, d_intra,
-        flops=1 << 30, n_bytes=4 << 20,
+        back, proj, te, d_intra, share,
+        flops=1 << 30, n_bytes=4 << 20, hbm=(4,),
     )
     part, attended = pl.pallas_call(
         share_sum_kernel,

time: 152 us -> 153 us (level)
  starting transfers between devices: 43.5 us -> 36.8 us
  Pallas kernels: 39 us -> 43.3 us
  local copies, waits for them, and re-layouts: 9.09 us -> 11.2 us
  blocking collectives: 15.7 us -> 13.6 us
    ppermute x3, starting transfers between devices: 13.7 us -> 7.59 us  [per_device(): met = lax.ppermute(part, 'dp', [(i, i ^ step) for i in range(dp)])]
    pallas_call x8 -> x9, Pallas kernels: 31.8 us -> 35 us  [call(): pl.pallas_call(kernel, out_shape=out_shape, in_specs=[smem if k < prefetc...]
    ppermute x1, starting transfers between devices: 6.06 us -> 3.23 us  [per_device(): other = lax.ppermute(mine, 'dp', pairs)]
    unnamed x29 -> x41, local copies, waits for them, and re-layouts: 8.91 us -> 11.1 us
    all_to_all x1, blocking collectives: 15.7 us -> 13.6 us  [exchange(): return lax.all_to_all(blocks, axis, split_axis=0, concat_axis=0, tiled=True)]
    ppermute x1, starting transfers between devices: 1.27 us -> 3.13 us  [per_device(): given = lax.ppermute(give, 'dp', pairs)]
  transfers between devices with their start and end apart: 9 -> 9, of which waited for: 6 -> 6; matrix products, arithmetic and copies ran while one was open for 0% -> 1% of each run, Pallas kernels for 17% -> 19%
where the time goes in v4:
time: 153 us; the launch traced here: 152 us
  Pallas kernels  43.3 us (28%)
  waiting for transfers between devices  42.8 us (28%)
  starting transfers between devices  36.8 us (24%)
  blocking collectives  13.6 us (9%)
  local copies, waits for them, and re-layouts  11.2 us (7%)
  other arithmetic  3.05 us (2%)
    all_to_all x4, waiting for transfers between devices, exchange(): return lax.all_to_all(blocks, axis, split_axis=0, concat_axis=0, tiled=True)  37.3 us
    pallas_call x9, Pallas kernels, call(): pl.pallas_call(kernel, out_shape=out_shape, in_specs=[smem if k < prefetc...  35 us
    all_to_all x4, starting transfers between devices, exchange(): return lax.all_to_all(blocks, axis, split_axis=0, concat_axis=0, tiled=True)  22.9 us
    all_to_all x1, blocking collectives, exchange(): return lax.all_to_all(blocks, axis, split_axis=0, concat_axis=0, tiled=True)  13.6 us
    unnamed x41, local copies, waits for them, and re-layouts  11.1 us
    ppermute x3, starting transfers between devices, per_device(): met = lax.ppermute(part, 'dp', [(i, i ^ step) for i in range(dp)])  7.59 us
    pallas_call x1, Pallas kernels, per_device(): pl.pallas_call(front_kernel, out_shape=(sds((ctx, 336, n_tok), bf16), sds...  7.12 us
    ppermute x1, starting transfers between devices, per_device(): other = lax.ppermute(mine, 'dp', pairs)  3.23 us
  transfers between devices with their start and end apart: 9, of which 6 were waited for; matrix products, arithmetic and copies ran while one was open for 1% of the time, Pallas kernels for 19%

profile of v4, /device:TPU:1, one launch (start us, length us, event | category | flops | bytes accessed | tf_op | source)
XLA Modules:
  0.0 151.7 jit_solution(14746411101524049380)
XLA Ops:
  0.6 7.1 %shard_map.102 = (bf16[16,336,256]{2,1,0:T(8,128)(2,1)}, bf16[256,256]{1,0:T(8,128)(2,1)}, bf16[256,32]{1,0:T(8,128)(2,1)}, bf16[256,32]{1,0:T(8,128)(2,1)}) custom-call(bf16[256,2048]{1,0:T(8,128)(2,1)} %bitcast.17, bf16[2048,256]{1,0:T(8,128)(2,1)} %w_hbm.1, bf16[256,2048]{1,0:T(8,128)(2,1)} %bitcast.19, bf16[256,2048]{1,0:T(8,128)(2,1)} %bitcast.21, ...), custom_call_target="tpu_custom_call" | custom-call | flops 2147483648 | bytes 9437184 | tf_op jit(solution)/shard_map/pallas_call | solution.py:387
  7.8 0.0 copy-start.6
  7.8 0.0 copy-start.7
  7.8 0.0 copy-start.12
  7.8 0.0 copy-start.14
  7.8 0.0 copy-start.18
  7.8 7.7 %all-to-all-start = ((bf16[16,336,256]{2,1,0:T(8,128)(2,1)}), bf16[16,336,256]{2,1,0:T(8,128)(2,1)S(1)}, u32[]{:S(2)}, u32[]{:S(2)}) async-start(bf16[16,336,256]{2,1,0:T(8,128)(2,1)} %get-tuple-element.24), calls=%async_computation | async-start | bytes 5505024 | tf_op jit(solution)/shard_map/all_to_all | solution.py:368
  15.6 0.0 copy-done.6
  15.6 0.0 copy-done.7
  15.6 0.0 copy-done.12
  15.6 0.0 copy-done.14
  15.6 0.0 copy-done.18
  15.6 0.0 copy-start.3
  15.6 1.2 copy-done.3
  16.8 0.0 copy-start.4
  16.8 1.2 copy-done.4
  18.1 1.2 copy-done.5
  19.3 4.6 %shard_map.103 = (f32[256,2048]{1,0:T(8,128)S(1)}, f32[256,256]{1,0:T(8,128)S(1)}, bf16[3,2048,256]{2,1,0:T(8,128)(2,1)S(1)}, f32[8,128]{1,0:T(8,128)S(1)}) custom-call(bf16[256,2048]{1,0:T(8,128)(2,1)S(1)} %bitcast.18, bf16[256,256]{1,0:T(8,128)(2,1)S(1)} %copy-done.12, bf16[256,2048]{1,0:T(8,128)(2,1)S(1)} %bitcast.20, bf16[256,2048]{1,0:T(8,128)(2,1)S(1)} %bitcast.22, ...), custom_call_target="tpu_custom_call" | custom-call | flops 6442450944 | bytes 8388608 | tf_op jit(solution)/shard_map/pallas_call | solution.py:49
  23.9 0.0 copy-start.10
  23.9 1.3 copy-done.10
  25.2 1.6 %copy-done.16 = bf16[3,2048,256]{2,1,0:T(8,128)(2,1)} copy-done((bf16[3,2048,256]{2,1,0:T(8,128)(2,1)}, bf16[3,2048,256]{2,1,0:T(8,128)(2,1)S(1)}, u32[]{:S(2)}) %copy-start.16) | copy-done | bytes 3145752
  26.8 0.7 copy-done.17
  27.5 28.8 %all-to-all-done.recv.qkv = bf16[16,336,256]{2,1,0:T(8,128)(2,1)S(1)} async-done(((bf16[16,336,256]{2,1,0:T(8,128)(2,1)}), bf16[16,336,256]{2,1,0:T(8,128)(2,1)S(1)}, u32[]{:S(2)}, u32[]{:S(2)}) %all-to-all-start) | async-done | bytes 2752544 | tf_op jit(solution)/shard_map/all_to_all | solution.py:368
  56.4 0.3 shard_map.104
  56.7 0.0 copy-start
  56.7 1.0 copy-done
  57.7 4.3 %all-to-all-start.1 = ((bf16[16,128,256]{2,1,0:T(8,128)(2,1)}), bf16[16,128,256]{2,1,0:T(8,128)(2,1)}, u32[]{:S(2)}, u32[]{:S(2)}) async-start(bf16[16,128,256]{2,1,0:T(8,128)(2,1)} %copy-done), calls=%async_computation.1 | async-start | bytes 2097152 | tf_op jit(solution)/shard_map/all_to_all | solution.py:368
  62.0 0.2 slice_reduce_fusion
  62.2 0.2 convert_reduce_fusion.lows.after
  62.4 10.7 %shard_map.105 = (bf16[10,64,256]{2,1,0:T(8,128)(2,1)S(1)}, f32[8,128]{1,0:T(8,128)S(1)}) custom-call(s32[16]{0:T(128)S(1)} %convert_reduce_fusion.lows.after, bf16[16,336,256]{2,1,0:T(8,128)(2,1)S(1)} %all-to-all-done.recv.qkv, s32[16]{0:T(128)S(1)} %convert_reduce_fusion.lows.after), custom_call_target="tpu_custom_call" | custom-call | flops 8589934592 | bytes 2097152 | tf_op jit(solution)/shard_map/pallas_call | solution.py:49
  73.1 0.0 copy-start.8
  73.1 0.5 copy-done.8
  73.6 0.6 copy-done.19
  74.2 3.1 %all-to-all-done.1.recv_hbm.recv = bf16[16,128,256]{2,1,0:T(8,128)(2,1)} async-done(((bf16[16,128,256]{2,1,0:T(8,128)(2,1)}), bf16[16,128,256]{2,1,0:T(8,128)(2,1)}, u32[]{:S(2)}, u32[]{:S(2)}) %all-to-all-start.1) | async-done | bytes 1048608 | tf_op jit(solution)/shard_map/all_to_all | solution.py:368
  77.3 4.6 %shard_map.106 = (bf16[256,256]{1,0:T(8,128)(2,1)}, bf16[16,64,256]{2,1,0:T(8,128)(2,1)}, bf16[16,64,256]{2,1,0:T(8,128)(2,1)}) custom-call(s32[1]{0:T(128)} %bitcast.8.core, bf16[16,128,256]{2,1,0:T(8,128)(2,1)} %all-to-all-done.1.recv_hbm.recv, bf16[3,2048,256]{2,1,0:T(8,128)(2,1)} %copy-done.16, f32[256,256]{1,0:T(8,128)} %copy-done.17, f32[8,128]{1,0:T(8,128)} %copy-done.19), custom_call_target="tpu_custom_call" | custom-call | flops 2147483648 | bytes 6291456 | tf_op jit(solution)/shard_map/pallas_call | solution.py:49
  81.9 3.1 %collective-permute-start = (bf16[16,64,256]{2,1,0:T(8,128)(2,1)}, bf16[16,64,256]{2,1,0:T(8,128)(2,1)S(1)}, u32[]{:S(2)}, u32[]{:S(2)}) collective-permute-start(bf16[16,64,256]{2,1,0:T(8,128)(2,1)} %get-tuple-element.34), channel_id=1, source_target_pairs={{0,16},{16,0},{32,48},{48,32},{64,80},{80,64},{96,112},{112,96},{1... | collective-permute-start | bytes 1572872 | tf_op jit(solution)/shard_map/ppermute | solution.py:457
  85.1 1.7 %collective-permute-done = bf16[16,64,256]{2,1,0:T(8,128)(2,1)S(1)} collective-permute-done((bf16[16,64,256]{2,1,0:T(8,128)(2,1)}, bf16[16,64,256]{2,1,0:T(8,128)(2,1)S(1)}, u32[]{:S(2)}, u32[]{:S(2)}) %collective-permute-start) | collective-permute-done | bytes 524320 | tf_op jit(solution)/shard_map/ppermute | solution.py:457
  86.8 2.0 %add_convert_fusion.after = bf16[16,64,256]{2,1,0:T(8,128)(2,1)} fusion(bf16[16,64,256]{2,1,0:T(8,128)(2,1)S(1)} %collective-permute-done, bf16[16,64,256]{2,1,0:T(8,128)(2,1)} %get-tuple-element.33), kind=kLoop, calls=%fused_computation | loop fusion | flops 1048576 | bytes 1572864 | tf_op jit(solution)/shard_map/convert_element_type | solution.py:458
  88.8 4.2 %all-to-all-start.2 = ((bf16[16,64,256]{2,1,0:T(8,128)(2,1)}), bf16[16,64,256]{2,1,0:T(8,128)(2,1)}, u32[]{:S(2)}, u32[]{:S(2)}) async-start(bf16[16,64,256]{2,1,0:T(8,128)(2,1)} %add_convert_fusion.after), calls=%async_computation.2 | async-start | bytes 1048576 | tf_op jit(solution)/shard_map/all_to_all | solution.py:368
  93.1 0.0 copy-start.1
  93.1 1.1 copy-done.1
  94.1 0.6 copy-done.9
  94.7 9.4 %shard_map.108 = (bf16[6,64,256]{2,1,0:T(8,128)(2,1)S(1)}, f32[8,128]{1,0:T(8,128)}) custom-call(s32[16]{0:T(128)S(1)} %copy-done.9, bf16[16,336,256]{2,1,0:T(8,128)(2,1)S(1)} %all-to-all-done.recv.qkv, bf16[16,64,256]{2,1,0:T(8,128)(2,1)S(1)} %copy-done.1), custom_call_target="tpu_custom_call" | custom-call | flops 8589934592 | bytes 2097152 | tf_op jit(solution)/shard_map/pallas_call | solution.py:49
  104.1 0.0 copy-done.2
  104.1 0.0 copy-done.11
  104.1 0.0 copy-done.13
  104.1 0.0 copy-done.15
  104.1 2.9 %shard_map.107 = (bf16[256,2048]{1,0:T(8,128)(2,1)}, f32[8,128]{1,0:T(8,128)S(1)}) custom-call(bf16[16,128,256]{2,1,0:T(8,128)(2,1)} %all-to-all-done.1.recv_hbm.recv, bf16[256,256]{1,0:T(8,128)(2,1)S(1)} %copy-done.13, bf16[256,32]{1,0:T(8,128)(2,1)S(1)} %copy-done.15, f32[256,2048]{1,0:T(8,128)S(1)} %copy-done.11, bf16[16,64,256]{2,1,0:T(8,128)(2,1)S(1)} %copy-done.2), custom_call_target="tpu_custom_call" | custom-call | flops 1073741824 | bytes 4194304 | tf_op jit(solution)/shard_map/pallas_call | solution.py:49
  107.0 0.8 pad_maximum_fusion.passed
  107.9 0.0 all-to-all-done.2.recv
  107.9 1.1 shard_map.109
  109.0 2.8 %collective-permute-start.1 = (bf16[64,256]{1,0:T(8,128)(2,1)S(1)}, bf16[64,256]{1,0:T(8,128)(2,1)S(1)}, u32[]{:S(2)}, u32[]{:S(2)}) collective-permute-start(bf16[64,256]{1,0:T(8,128)(2,1)S(1)} %get-tuple-element.40), channel_id=1, source_target_pairs={{0,32},{16,48},{32,0},{48,16},{64,96},{80,112},{96,64},{112,80},{1... | collective-permute-start | bytes 98312 | tf_op jit(solution)/shard_map/ppermute | solution.py:482
  111.8 6.5 %all-to-all-start.3 = ((bf16[16,64,256]{2,1,0:T(8,128)(2,1)}), bf16[16,64,256]{2,1,0:T(8,128)(2,1)S(1)}, u32[]{:S(2)}, u32[]{:S(2)}) async-start(bf16[16,64,256]{2,1,0:T(8,128)(2,1)} %get-tuple-element.41), calls=%async_computation.3 | async-start | bytes 1048576 | tf_op jit(solution)/shard_map/all_to_all | solution.py:368
  118.3 0.0 collective-permute-done.1
  118.3 2.2 %collective-permute-start.2 = (bf16[64,256]{1,0:T(8,128)(2,1)S(1)}, bf16[64,256]{1,0:T(8,128)(2,1)S(1)}, u32[]{:S(2)}, u32[]{:S(2)}) collective-permute-start(bf16[64,256]{1,0:T(8,128)(2,1)S(1)} %add_convert_fusion.2), channel_id=1, source_target_pairs={{0,64},{16,80},{32,96},{48,112},{64,0},{80,16},{96,32},{112,48},{1... | collective-permute-start | bytes 98312 | tf_op jit(solution)/shard_map/ppermute | solution.py:482
  120.5 2.1 %collective-permute-done.2 = bf16[64,256]{1,0:T(8,128)(2,1)S(1)} collective-permute-done((bf16[64,256]{1,0:T(8,128)(2,1)S(1)}, bf16[64,256]{1,0:T(8,128)(2,1)S(1)}, u32[]{:S(2)}, u32[]{:S(2)}) %collective-permute-start.2) | collective-permute-done | bytes 32800 | tf_op jit(solution)/shard_map/ppermute | solution.py:482
  122.7 2.6 %collective-permute-start.3 = (bf16[64,256]{1,0:T(8,128)(2,1)S(1)}, bf16[64,256]{1,0:T(8,128)(2,1)S(1)}, u32[]{:S(2)}, u32[]{:S(2)}) collective-permute-start(bf16[64,256]{1,0:T(8,128)(2,1)S(1)} %add_convert_fusion.1.part), channel_id=1, source_target_pairs={{0,128},{16,144},{32,160},{48,176},{64,192},{80,208},{96,224},{112... | collective-permute-start | bytes 98312 | tf_op jit(solution)/shard_map/ppermute | solution.py:485
  125.3 5.4 %all-to-all-done.3.recv = bf16[16,64,256]{2,1,0:T(8,128)(2,1)S(1)} async-done(((bf16[16,64,256]{2,1,0:T(8,128)(2,1)}), bf16[16,64,256]{2,1,0:T(8,128)(2,1)S(1)}, u32[]{:S(2)}, u32[]{:S(2)}) %all-to-all-start.3) | async-done | bytes 524320 | tf_op jit(solution)/shard_map/all_to_all | solution.py:368
  130.8 1.0 shard_map.110
  131.8 0.0 collective-permute-done.3.met
  131.8 13.6 %all_to_all.25.mine = bf16[16,64,256]{2,1,0:T(8,128)(2,1)S(1)} all-to-all(bf16[16,64,256]{2,1,0:T(8,128)(2,1)S(1)} %shard_map.111), channel_id=1, replica_groups=mesh['dp'=16,'ctx'=16] {'ctx'}, dimensions={0} | all-to-all | bytes 1048576 | tf_op jit(solution)/shard_map/all_to_all | solution.py:368
  145.4 3.2 %collective-permute-start.4 = (bf16[16,64,256]{2,1,0:T(8,128)(2,1)S(1)}, bf16[16,64,256]{2,1,0:T(8,128)(2,1)S(1)}, u32[]{:S(2)}, u32[]{:S(2)}) collective-permute-start(bf16[16,64,256]{2,1,0:T(8,128)(2,1)S(1)} %all_to_all.25.mine), channel_id=1, source_target_pairs={{0,16},{16,0},{32,48},{48,32},{64,80},{80,64},{96,112},{112,96},{1... | collective-permute-start | bytes 1572872 | tf_op jit(solution)/shard_map/ppermute | solution.py:488
  148.7 1.5 %collective-permute-done.4.other = bf16[16,64,256]{2,1,0:T(8,128)(2,1)S(1)} collective-permute-done((bf16[16,64,256]{2,1,0:T(8,128)(2,1)S(1)}, bf16[16,64,256]{2,1,0:T(8,128)(2,1)S(1)}, u32[]{:S(2)}, u32[]{:S(2)}) %collective-permute-start.4) | collective-permute-done | bytes 524320 | tf_op jit(solution)/shard_map/ppermute | solution.py:488
  150.2 1.5 shard_map.112
  (14 shorter events, 0.1 us)
Async XLA Ops:
  7.8 7.8 %copy-start.6 = (bf16[1,256,32]{1,2,0:T(8,128)(2,1)S(1)}, bf16[1,256,32]{1,2,0:T(8,128)(2,1)}, u32[]{:S(2)}) copy-start(bf16[1,256,32]{1,2,0:T(8,128)(2,1)} %param.10) | copy-start | bytes 49156
  7.8 7.8 %copy-start.7 = (s32[1,256]{1,0:T(1,128)S(1)}, s32[1,256]{1,0:T(1,128)}, u32[]{:S(2)}) copy-start(s32[1,256]{1,0:T(1,128)} %ids.1) | copy-start | bytes 3076
  7.8 7.8 %copy-start.12 = (bf16[256,256]{1,0:T(8,128)(2,1)S(1)}, bf16[256,256]{1,0:T(8,128)(2,1)}, u32[]{:S(2)}) copy-start(bf16[256,256]{1,0:T(8,128)(2,1)} %get-tuple-element.25.proj) | copy-start | bytes 393220
  7.8 7.8 %copy-start.14 = (bf16[256,32]{1,0:T(8,128)(2,1)S(1)}, bf16[256,32]{1,0:T(8,128)(2,1)}, u32[]{:S(2)}) copy-start(bf16[256,32]{1,0:T(8,128)(2,1)} %get-tuple-element.26.te) | copy-start | bytes 49156
  7.8 7.8 %copy-start.18 = (bf16[256,32]{1,0:T(8,128)(2,1)S(1)}, bf16[256,32]{1,0:T(8,128)(2,1)}, u32[]{:S(2)}) copy-start(bf16[256,32]{1,0:T(8,128)(2,1)} %get-tuple-element.27.fs) | copy-start | bytes 49156
  7.8 48.5 %all-to-all-start = ((bf16[16,336,256]{2,1,0:T(8,128)(2,1)}), bf16[16,336,256]{2,1,0:T(8,128)(2,1)S(1)}, u32[]{:S(2)}, u32[]{:S(2)}) async-start(bf16[16,336,256]{2,1,0:T(8,128)(2,1)} %get-tuple-element.24), calls=%async_computation | async-start | bytes 5505024 | tf_op jit(solution)/shard_map/all_to_all | solution.py:368
  15.6 1.2 copy-start.3
  16.8 1.2 copy-start.4
  18.1 1.2 copy-start.5
  23.9 1.3 copy-start.10
  25.2 1.6 %copy-start.16 = (bf16[3,2048,256]{2,1,0:T(8,128)(2,1)}, bf16[3,2048,256]{2,1,0:T(8,128)(2,1)S(1)}, u32[]{:S(2)}) copy-start(bf16[3,2048,256]{2,1,0:T(8,128)(2,1)S(1)} %get-tuple-element.30.kept_hbm) | copy-start | bytes 9437188
  26.8 0.7 copy-start.17
  56.7 1.0 copy-start
  57.7 19.6 %all-to-all-start.1 = ((bf16[16,128,256]{2,1,0:T(8,128)(2,1)}), bf16[16,128,256]{2,1,0:T(8,128)(2,1)}, u32[]{:S(2)}, u32[]{:S(2)}) async-start(bf16[16,128,256]{2,1,0:T(8,128)(2,1)} %copy-done), calls=%async_computation.1 | async-start | bytes 2097152 | tf_op jit(solution)/shard_map/all_to_all | solution.py:368
  73.1 0.5 copy-start.8
  73.6 0.6 copy-start.19
  81.9 4.9 %collective-permute-start = (bf16[16,64,256]{2,1,0:T(8,128)(2,1)}, bf16[16,64,256]{2,1,0:T(8,128)(2,1)S(1)}, u32[]{:S(2)}, u32[]{:S(2)}) collective-permute-start(bf16[16,64,256]{2,1,0:T(8,128)(2,1)} %get-tuple-element.34), channel_id=1, source_target_pairs={{0,16},{16,0},{32,48},{48,32},{64,80},{80,64},{96,112},{112,96},{1... | collective-permute-start | bytes 1572872 | tf_op jit(solution)/shard_map/ppermute | solution.py:457
  88.8 19.1 %all-to-all-start.2 = ((bf16[16,64,256]{2,1,0:T(8,128)(2,1)}), bf16[16,64,256]{2,1,0:T(8,128)(2,1)}, u32[]{:S(2)}, u32[]{:S(2)}) async-start(bf16[16,64,256]{2,1,0:T(8,128)(2,1)} %add_convert_fusion.after), calls=%async_computation.2 | async-start | bytes 1048576 | tf_op jit(solution)/shard_map/all_to_all | solution.py:368
  93.1 1.1 copy-start.1
  94.1 0.6 copy-start.9
  94.7 9.4 %copy-start.2 = (bf16[16,64,256]{2,1,0:T(8,128)(2,1)S(1)}, bf16[16,64,256]{2,1,0:T(8,128)(2,1)}, u32[]{:S(2)}) copy-start(bf16[16,64,256]{2,1,0:T(8,128)(2,1)} %add_convert_fusion.after) | copy-start | bytes 1572868
  94.7 9.4 %copy-start.11 = (f32[256,2048]{1,0:T(8,128)S(1)}, f32[256,2048]{1,0:T(8,128)}, u32[]{:S(2)}) copy-start(f32[256,2048]{1,0:T(8,128)} %copy-done.10) | copy-start | bytes 6291460
  94.7 9.4 %copy-start.13 = (bf16[256,256]{1,0:T(8,128)(2,1)S(1)}, bf16[256,256]{1,0:T(8,128)(2,1)}, u32[]{:S(2)}) copy-start(bf16[256,256]{1,0:T(8,128)(2,1)} %get-tuple-element.25.proj) | copy-start | bytes 393220
  94.7 9.4 %copy-start.15 = (bf16[256,32]{1,0:T(8,128)(2,1)S(1)}, bf16[256,32]{1,0:T(8,128)(2,1)}, u32[]{:S(2)}) copy-start(bf16[256,32]{1,0:T(8,128)(2,1)} %get-tuple-element.26.te) | copy-start | bytes 49156
  109.0 9.3 %collective-permute-start.1 = (bf16[64,256]{1,0:T(8,128)(2,1)S(1)}, bf16[64,256]{1,0:T(8,128)(2,1)S(1)}, u32[]{:S(2)}, u32[]{:S(2)}) collective-permute-start(bf16[64,256]{1,0:T(8,128)(2,1)S(1)} %get-tuple-element.40), channel_id=1, source_target_pairs={{0,32},{16,48},{32,0},{48,16},{64,96},{80,112},{96,64},{112,80},{1... | collective-permute-start | bytes 98312 | tf_op jit(solution)/shard_map/ppermute | solution.py:482
  111.8 19.0 %all-to-all-start.3 = ((bf16[16,64,256]{2,1,0:T(8,128)(2,1)}), bf16[16,64,256]{2,1,0:T(8,128)(2,1)S(1)}, u32[]{:S(2)}, u32[]{:S(2)}) async-start(bf16[16,64,256]{2,1,0:T(8,128)(2,1)} %get-tuple-element.41), calls=%async_computation.3 | async-start | bytes 1048576 | tf_op jit(solution)/shard_map/all_to_all | solution.py:368
  118.3 4.3 %collective-permute-start.2 = (bf16[64,256]{1,0:T(8,128)(2,1)S(1)}, bf16[64,256]{1,0:T(8,128)(2,1)S(1)}, u32[]{:S(2)}, u32[]{:S(2)}) collective-permute-start(bf16[64,256]{1,0:T(8,128)(2,1)S(1)} %add_convert_fusion.2), channel_id=1, source_target_pairs={{0,64},{16,80},{32,96},{48,112},{64,0},{80,16},{96,32},{112,48},{1... | collective-permute-start | bytes 98312 | tf_op jit(solution)/shard_map/ppermute | solution.py:482
  122.7 9.1 %collective-permute-start.3 = (bf16[64,256]{1,0:T(8,128)(2,1)S(1)}, bf16[64,256]{1,0:T(8,128)(2,1)S(1)}, u32[]{:S(2)}, u32[]{:S(2)}) collective-permute-start(bf16[64,256]{1,0:T(8,128)(2,1)S(1)} %add_convert_fusion.1.part), channel_id=1, source_target_pairs={{0,128},{16,144},{32,160},{48,176},{64,192},{80,208},{96,224},{112... | collective-permute-start | bytes 98312 | tf_op jit(solution)/shard_map/ppermute | solution.py:485
  145.4 4.8 %collective-permute-start.4 = (bf16[16,64,256]{2,1,0:T(8,128)(2,1)S(1)}, bf16[16,64,256]{2,1,0:T(8,128)(2,1)S(1)}, u32[]{:S(2)}, u32[]{:S(2)}) collective-permute-start(bf16[16,64,256]{2,1,0:T(8,128)(2,1)S(1)} %all_to_all.25.mine), channel_id=1, source_target_pairs={{0,16},{16,0},{32,48},{48,32},{64,80},{80,64},{96,112},{112,96},{1... | collective-permute-start | bytes 1572872 | tf_op jit(solution)/shard_map/ppermute | solution.py:488

commit v5 on v4

--- a/solution.py
+++ b/solution.py
@@ -439,7 +439,7 @@
             flops=8 << 30, n_bytes=2 << 20, prefetch=1, hbm=(2,),
         )
 
-    split = ctx * 5 // 16 * 2
+    split = ctx * 3 // 8 * 2
     attended, attention_done = attend(0, split, lows)
 
     half_rows = width // ctx // 2
@@ -457,11 +457,11 @@
     given = lax.ppermute(give, "dp", pairs)
     share = (keep.astype(f32) + given.astype(f32)).astype(bf16)
     shares = exchange(share, "ctx")
-    attended = jnp.concatenate([attended, attend(split, ctx, share)[0]])
+    attended = jnp.concatenate([attended, attend(split, ctx, share[0, :8, :128])[0]])
     input_grad, input_done = call(
         input_grad_kernel,
         (sds((n_tok, width), bf16), done),
-        back, proj, te, d_intra, share,
+        back, proj, te, d_intra, share[0, :8, :128],
         flops=1 << 30, n_bytes=4 << 20, hbm=(4,),
     )
     part, attended = pl.pallas_call(

time: 153 us -> 151 us (0.987)
  starting transfers between devices: 36.8 us -> 42.7 us
  waiting for transfers between devices: 42.8 us -> 38.1 us
  Pallas kernels: 43.3 us -> 40.4 us
    all_to_all x4, waiting for transfers between devices: 37.3 us -> 33.3 us  [exchange(): return lax.all_to_all(blocks, axis, split_axis=0, concat_axis=0, tiled=True)]
    ppermute x1, starting transfers between devices: 3.23 us -> 6.53 us  [per_device(): other = lax.ppermute(mine, 'dp', pairs)]
    pallas_call x9, Pallas kernels: 35 us -> 32.1 us  [call(): pl.pallas_call(kernel, out_shape=out_shape, in_specs=[smem if k < prefetc...]
    ppermute x3, starting transfers between devices: 7.59 us -> 10.2 us  [per_device(): met = lax.ppermute(part, 'dp', [(i, i ^ step) for i in range(dp)])]
    unnamed x41 -> x33, local copies, waits for them, and re-layouts: 11.1 us -> 9.64 us
  transfers between devices with their start and end apart: 9 -> 9, of which waited for: 6 -> 6; matrix products, arithmetic and copies ran while one was open for 1% -> 1% of each run, Pallas kernels for 19% -> 17%
where the time goes in v5:
time: 151 us
  starting transfers between devices  42.7 us (28%)
  Pallas kernels  40.4 us (27%)
  waiting for transfers between devices  38.1 us (25%)
  blocking collectives  15.1 us (10%)
  local copies, waits for them, and re-layouts  10.5 us (7%)
  other arithmetic  3.05 us (2%)
    all_to_all x4, waiting for transfers between devices, exchange(): return lax.all_to_all(blocks, axis, split_axis=0, concat_axis=0, tiled=True)  33.3 us
    pallas_call x9, Pallas kernels, call(): pl.pallas_call(kernel, out_shape=out_shape, in_specs=[smem if k < prefetc...  32.1 us
    all_to_all x4, starting transfers between devices, exchange(): return lax.all_to_all(blocks, axis, split_axis=0, concat_axis=0, tiled=True)  22.8 us
    all_to_all x1, blocking collectives, exchange(): return lax.all_to_all(blocks, axis, split_axis=0, concat_axis=0, tiled=True)  15.1 us
    ppermute x3, starting transfers between devices, per_device(): met = lax.ppermute(part, 'dp', [(i, i ^ step) for i in range(dp)])  10.2 us
    unnamed x33, local copies, waits for them, and re-layouts  9.64 us
    pallas_call x1, Pallas kernels, per_device(): pl.pallas_call(front_kernel, out_shape=(sds((ctx, 336, n_tok), bf16), sds...  7.12 us
    ppermute x1, starting transfers between devices, per_device(): other = lax.ppermute(mine, 'dp', pairs)  6.53 us
  transfers between devices with their start and end apart: 9, of which 6 were waited for; matrix products, arithmetic and copies ran while one was open for 1% of the time, Pallas kernels for 17%

profile of v5, /device:TPU:1, one launch (start us, length us, event | category | flops | bytes accessed | tf_op | source)
XLA Modules:
  0.0 150.7 jit_solution(10249153901199778281)
XLA Ops:
  0.6 7.1 %shard_map.102 = (bf16[16,336,256]{2,1,0:T(8,128)(2,1)}, bf16[256,256]{1,0:T(8,128)(2,1)}, bf16[256,32]{1,0:T(8,128)(2,1)}, bf16[256,32]{1,0:T(8,128)(2,1)}) custom-call(bf16[256,2048]{1,0:T(8,128)(2,1)} %bitcast.19, bf16[2048,256]{1,0:T(8,128)(2,1)} %w_hbm.1, bf16[256,2048]{1,0:T(8,128)(2,1)} %bitcast.21, bf16[256,2048]{1,0:T(8,128)(2,1)} %bitcast.23, ...), custom_call_target="tpu_custom_call" | custom-call | flops 2147483648 | bytes 9437184 | tf_op jit(solution)/shard_map/pallas_call | solution.py:387
  7.8 0.0 copy-start.6
  7.8 0.0 copy-start.7
  7.8 0.0 copy-start.10
  7.8 0.0 copy-start.12
  7.8 0.0 copy-start.14
  7.8 7.7 %all-to-all-start = ((bf16[16,336,256]{2,1,0:T(8,128)(2,1)}), bf16[16,336,256]{2,1,0:T(8,128)(2,1)S(1)}, u32[]{:S(2)}, u32[]{:S(2)}) async-start(bf16[16,336,256]{2,1,0:T(8,128)(2,1)} %get-tuple-element.24), calls=%async_computation | async-start | bytes 5505024 | tf_op jit(solution)/shard_map/all_to_all | solution.py:368
  15.6 0.0 copy-done.6
  15.6 0.0 copy-done.7
  15.6 0.0 copy-done.10
  15.6 0.0 copy-done.12
  15.6 0.0 copy-done.14
  15.6 0.0 copy-start.3
  15.6 1.2 copy-done.3
  16.8 0.0 copy-start.4
  16.9 1.2 copy-done.4
  18.1 1.2 copy-done.5
  19.3 4.6 %shard_map.103 = (f32[256,2048]{1,0:T(8,128)S(1)}, f32[256,256]{1,0:T(8,128)S(1)}, bf16[3,2048,256]{2,1,0:T(8,128)(2,1)S(1)}, f32[8,128]{1,0:T(8,128)S(1)}) custom-call(bf16[256,2048]{1,0:T(8,128)(2,1)S(1)} %bitcast.20, bf16[256,256]{1,0:T(8,128)(2,1)S(1)} %copy-done.10, bf16[256,2048]{1,0:T(8,128)(2,1)S(1)} %bitcast.22, bf16[256,2048]{1,0:T(8,128)(2,1)S(1)} %bitcast.24, ...), custom_call_target="tpu_custom_call" | custom-call | flops 6442450944 | bytes 8388608 | tf_op jit(solution)/shard_map/pallas_call | solution.py:49
  23.9 0.0 copy-start.8
  23.9 1.3 copy-done.8
  25.2 0.0 copy-start.11
  25.2 1.6 %copy-done.11 = bf16[3,2048,256]{2,1,0:T(8,128)(2,1)} copy-done((bf16[3,2048,256]{2,1,0:T(8,128)(2,1)}, bf16[3,2048,256]{2,1,0:T(8,128)(2,1)S(1)}, u32[]{:S(2)}) %copy-start.11) | copy-done | bytes 3145752
  26.9 0.0 copy-start.13
  26.9 0.7 copy-done.13
  27.5 28.8 %all-to-all-done.recv.qkv = bf16[16,336,256]{2,1,0:T(8,128)(2,1)S(1)} async-done(((bf16[16,336,256]{2,1,0:T(8,128)(2,1)}), bf16[16,336,256]{2,1,0:T(8,128)(2,1)S(1)}, u32[]{:S(2)}, u32[]{:S(2)}) %all-to-all-start) | async-done | bytes 2752544 | tf_op jit(solution)/shard_map/all_to_all | solution.py:368
  56.4 0.3 shard_map.104
  56.7 0.0 copy-start
  56.7 1.0 copy-done
  57.7 4.3 %all-to-all-start.1 = ((bf16[16,128,256]{2,1,0:T(8,128)(2,1)}), bf16[16,128,256]{2,1,0:T(8,128)(2,1)}, u32[]{:S(2)}, u32[]{:S(2)}) async-start(bf16[16,128,256]{2,1,0:T(8,128)(2,1)} %copy-done), calls=%async_computation.1 | async-start | bytes 2097152 | tf_op jit(solution)/shard_map/all_to_all | solution.py:368
  62.0 0.2 slice_reduce_fusion
  62.2 0.2 convert_reduce_fusion.lows.after
  62.4 9.9 %shard_map.105 = (bf16[12,64,256]{2,1,0:T(8,128)(2,1)S(1)}, f32[8,128]{1,0:T(8,128)S(1)}) custom-call(s32[16]{0:T(128)S(1)} %convert_reduce_fusion.lows.after, bf16[16,336,256]{2,1,0:T(8,128)(2,1)S(1)} %all-to-all-done.recv.qkv, s32[16]{0:T(128)S(1)} %convert_reduce_fusion.lows.after), custom_call_target="tpu_custom_call" | custom-call | flops 8589934592 | bytes 2097152 | tf_op jit(solution)/shard_map/pallas_call | solution.py:49
  72.3 0.0 copy-start.1
  72.3 0.7 copy-done.1
  73.1 0.0 copy-start.15
  73.1 0.6 copy-done.15
  73.7 3.6 %all-to-all-done.1.recv_hbm.recv = bf16[16,128,256]{2,1,0:T(8,128)(2,1)} async-done(((bf16[16,128,256]{2,1,0:T(8,128)(2,1)}), bf16[16,128,256]{2,1,0:T(8,128)(2,1)}, u32[]{:S(2)}, u32[]{:S(2)}) %all-to-all-start.1) | async-done | bytes 1048608 | tf_op jit(solution)/shard_map/all_to_all | solution.py:368
  77.3 4.6 %shard_map.106 = (bf16[256,256]{1,0:T(8,128)(2,1)}, bf16[16,64,256]{2,1,0:T(8,128)(2,1)}, bf16[16,64,256]{2,1,0:T(8,128)(2,1)}) custom-call(s32[1]{0:T(128)} %bitcast.8.core, bf16[16,128,256]{2,1,0:T(8,128)(2,1)} %all-to-all-done.1.recv_hbm.recv, bf16[3,2048,256]{2,1,0:T(8,128)(2,1)} %copy-done.11, f32[256,256]{1,0:T(8,128)} %copy-done.13, f32[8,128]{1,0:T(8,128)} %copy-done.15), custom_call_target="tpu_custom_call" | custom-call | flops 2147483648 | bytes 6291456 | tf_op jit(solution)/shard_map/pallas_call | solution.py:49
  81.9 3.1 %collective-permute-start = (bf16[16,64,256]{2,1,0:T(8,128)(2,1)}, bf16[16,64,256]{2,1,0:T(8,128)(2,1)S(1)}, u32[]{:S(2)}, u32[]{:S(2)}) collective-permute-start(bf16[16,64,256]{2,1,0:T(8,128)(2,1)} %get-tuple-element.34), channel_id=1, source_target_pairs={{0,16},{16,0},{32,48},{48,32},{64,80},{80,64},{96,112},{112,96},{1... | collective-permute-start | bytes 1572872 | tf_op jit(solution)/shard_map/ppermute | solution.py:457
  85.1 1.7 %collective-permute-done = bf16[16,64,256]{2,1,0:T(8,128)(2,1)S(1)} collective-permute-done((bf16[16,64,256]{2,1,0:T(8,128)(2,1)}, bf16[16,64,256]{2,1,0:T(8,128)(2,1)S(1)}, u32[]{:S(2)}, u32[]{:S(2)}) %collective-permute-start) | collective-permute-done | bytes 524320 | tf_op jit(solution)/shard_map/ppermute | solution.py:457
  86.8 2.0 %add_convert_fusion = bf16[16,64,256]{2,1,0:T(8,128)(2,1)} fusion(bf16[16,64,256]{2,1,0:T(8,128)(2,1)S(1)} %collective-permute-done, bf16[16,64,256]{2,1,0:T(8,128)(2,1)} %get-tuple-element.33), kind=kLoop, calls=%fused_computation | loop fusion | flops 1048576 | bytes 1572864 | tf_op jit(solution)/shard_map/convert_element_type | solution.py:458
  88.8 0.7 slice_bitcast_fusion.after
  89.5 4.2 %all-to-all-start.2 = ((bf16[16,64,256]{2,1,0:T(8,128)(2,1)}), bf16[16,64,256]{2,1,0:T(8,128)(2,1)}, u32[]{:S(2)}, u32[]{:S(2)}) async-start(bf16[16,64,256]{2,1,0:T(8,128)(2,1)} %add_convert_fusion), calls=%async_computation.2 | async-start | bytes 1048576 | tf_op jit(solution)/shard_map/all_to_all | solution.py:368
  93.7 0.0 copy-start.9
  93.8 7.2 %shard_map.108 = (bf16[4,64,256]{2,1,0:T(8,128)(2,1)S(1)}, f32[8,128]{1,0:T(8,128)}) custom-call(s32[16]{0:T(128)S(1)} %convert_reduce_fusion.lows.after, bf16[16,336,256]{2,1,0:T(8,128)(2,1)S(1)} %all-to-all-done.recv.qkv, bf16[8,128]{1,0:T(8,128)(2,1)S(1)} %slice_bitcast_fusion.after), custom_call_target="tpu_custom_call" | custom-call | flops 8589934592 | bytes 2097152 | tf_op jit(solution)/shard_map/pallas_call | solution.py:49
  100.9 0.0 copy-done.9
  100.9 2.9 %shard_map.107 = (bf16[256,2048]{1,0:T(8,128)(2,1)}, f32[8,128]{1,0:T(8,128)S(1)}) custom-call(bf16[16,128,256]{2,1,0:T(8,128)(2,1)} %all-to-all-done.1.recv_hbm.recv, bf16[256,256]{1,0:T(8,128)(2,1)S(1)} %copy-done.10, bf16[256,32]{1,0:T(8,128)(2,1)S(1)} %copy-done.12, f32[256,2048]{1,0:T(8,128)S(1)} %copy-done.9, bf16[8,128]{1,0:T(8,128)(2,1)S(1)} %slice_bitcast_fusion.after), custom_call_target="tpu_custom_call" | custom-call | flops 1073741824 | bytes 4194304 | tf_op jit(solution)/shard_map/pallas_call | solution.py:49
  103.9 0.0 copy-done.2
  103.9 0.8 pad_maximum_fusion.passed
  104.7 0.0 all-to-all-done.2.recv
  104.7 1.1 shard_map.109
  105.9 2.1 %collective-permute-start.1 = (bf16[64,256]{1,0:T(8,128)(2,1)S(1)}, bf16[64,256]{1,0:T(8,128)(2,1)S(1)}, u32[]{:S(2)}, u32[]{:S(2)}) collective-permute-start(bf16[64,256]{1,0:T(8,128)(2,1)S(1)} %get-tuple-element.40), channel_id=1, source_target_pairs={{0,32},{16,48},{32,0},{48,16},{64,96},{80,112},{96,64},{112,80},{1... | collective-permute-start | bytes 98312 | tf_op jit(solution)/shard_map/ppermute | solution.py:482
  107.9 6.5 %all-to-all-start.3 = ((bf16[16,64,256]{2,1,0:T(8,128)(2,1)}), bf16[16,64,256]{2,1,0:T(8,128)(2,1)S(1)}, u32[]{:S(2)}, u32[]{:S(2)}) async-start(bf16[16,64,256]{2,1,0:T(8,128)(2,1)} %get-tuple-element.41), calls=%async_computation.3 | async-start | bytes 1048576 | tf_op jit(solution)/shard_map/all_to_all | solution.py:368
  114.5 0.0 collective-permute-done.1
  114.5 2.3 %collective-permute-start.2 = (bf16[64,256]{1,0:T(8,128)(2,1)S(1)}, bf16[64,256]{1,0:T(8,128)(2,1)S(1)}, u32[]{:S(2)}, u32[]{:S(2)}) collective-permute-start(bf16[64,256]{1,0:T(8,128)(2,1)S(1)} %add_convert_fusion.2), channel_id=1, source_target_pairs={{0,64},{16,80},{32,96},{48,112},{64,0},{80,16},{96,32},{112,48},{1... | collective-permute-start | bytes 98312 | tf_op jit(solution)/shard_map/ppermute | solution.py:482
  116.8 1.5 collective-permute-done.2
  118.3 5.8 %collective-permute-start.3 = (bf16[64,256]{1,0:T(8,128)(2,1)S(1)}, bf16[64,256]{1,0:T(8,128)(2,1)S(1)}, u32[]{:S(2)}, u32[]{:S(2)}) collective-permute-start(bf16[64,256]{1,0:T(8,128)(2,1)S(1)} %add_convert_fusion.1.part), channel_id=1, source_target_pairs={{0,128},{16,144},{32,160},{48,176},{64,192},{80,208},{96,224},{112... | collective-permute-start | bytes 98312 | tf_op jit(solution)/shard_map/ppermute | solution.py:485
  124.1 0.9 all-to-all-done.3.recv
  125.0 1.0 shard_map.110
  126.0 0.0 collective-permute-done.3.met
  126.1 15.1 %all_to_all.25.mine = bf16[16,64,256]{2,1,0:T(8,128)(2,1)S(1)} all-to-all(bf16[16,64,256]{2,1,0:T(8,128)(2,1)S(1)} %shard_map.111), channel_id=1, replica_groups=mesh['dp'=16,'ctx'=16] {'ctx'}, dimensions={0} | all-to-all | bytes 1048576 | tf_op jit(solution)/shard_map/all_to_all | solution.py:368
  141.2 6.5 %collective-permute-start.4 = (bf16[16,64,256]{2,1,0:T(8,128)(2,1)S(1)}, bf16[16,64,256]{2,1,0:T(8,128)(2,1)S(1)}, u32[]{:S(2)}, u32[]{:S(2)}) collective-permute-start(bf16[16,64,256]{2,1,0:T(8,128)(2,1)S(1)} %all_to_all.25.mine), channel_id=1, source_target_pairs={{0,16},{16,0},{32,48},{48,32},{64,80},{80,64},{96,112},{112,96},{1... | collective-permute-start | bytes 1572872 | tf_op jit(solution)/shard_map/ppermute | solution.py:488
  147.7 1.5 %collective-permute-done.4.other = bf16[16,64,256]{2,1,0:T(8,128)(2,1)S(1)} collective-permute-done((bf16[16,64,256]{2,1,0:T(8,128)(2,1)S(1)}, bf16[16,64,256]{2,1,0:T(8,128)(2,1)S(1)}, u32[]{:S(2)}, u32[]{:S(2)}) %collective-permute-start.4) | collective-permute-done | bytes 524320 | tf_op jit(solution)/shard_map/ppermute | solution.py:488
  149.3 1.5 shard_map.112
  (7 shorter events, 0.1 us)
Async XLA Ops:
  7.8 7.8 %copy-start.6 = (bf16[1,256,32]{1,2,0:T(8,128)(2,1)S(1)}, bf16[1,256,32]{1,2,0:T(8,128)(2,1)}, u32[]{:S(2)}) copy-start(bf16[1,256,32]{1,2,0:T(8,128)(2,1)} %param.10) | copy-start | bytes 49156
  7.8 7.8 %copy-start.7 = (s32[1,256]{1,0:T(1,128)S(1)}, s32[1,256]{1,0:T(1,128)}, u32[]{:S(2)}) copy-start(s32[1,256]{1,0:T(1,128)} %ids.1) | copy-start | bytes 3076
  7.8 7.8 %copy-start.10 = (bf16[256,256]{1,0:T(8,128)(2,1)S(1)}, bf16[256,256]{1,0:T(8,128)(2,1)}, u32[]{:S(2)}) copy-start(bf16[256,256]{1,0:T(8,128)(2,1)} %get-tuple-element.25.proj) | copy-start | bytes 393220
  7.8 7.8 %copy-start.12 = (bf16[256,32]{1,0:T(8,128)(2,1)S(1)}, bf16[256,32]{1,0:T(8,128)(2,1)}, u32[]{:S(2)}) copy-start(bf16[256,32]{1,0:T(8,128)(2,1)} %get-tuple-element.26.te) | copy-start | bytes 49156
  7.8 7.8 %copy-start.14 = (bf16[256,32]{1,0:T(8,128)(2,1)S(1)}, bf16[256,32]{1,0:T(8,128)(2,1)}, u32[]{:S(2)}) copy-start(bf16[256,32]{1,0:T(8,128)(2,1)} %get-tuple-element.27.fs) | copy-start | bytes 49156
  7.8 48.5 %all-to-all-start = ((bf16[16,336,256]{2,1,0:T(8,128)(2,1)}), bf16[16,336,256]{2,1,0:T(8,128)(2,1)S(1)}, u32[]{:S(2)}, u32[]{:S(2)}) async-start(bf16[16,336,256]{2,1,0:T(8,128)(2,1)} %get-tuple-element.24), calls=%async_computation | async-start | bytes 5505024 | tf_op jit(solution)/shard_map/all_to_all | solution.py:368
  15.6 1.2 copy-start.3
  16.8 1.2 copy-start.4
  18.1 1.2 copy-start.5
  23.9 1.3 copy-start.8
  25.2 1.6 %copy-start.11 = (bf16[3,2048,256]{2,1,0:T(8,128)(2,1)}, bf16[3,2048,256]{2,1,0:T(8,128)(2,1)S(1)}, u32[]{:S(2)}) copy-start(bf16[3,2048,256]{2,1,0:T(8,128)(2,1)S(1)} %get-tuple-element.30.kept_hbm) | copy-start | bytes 9437188
  26.9 0.7 copy-start.13
  56.7 1.0 copy-start
  57.7 19.6 %all-to-all-start.1 = ((bf16[16,128,256]{2,1,0:T(8,128)(2,1)}), bf16[16,128,256]{2,1,0:T(8,128)(2,1)}, u32[]{:S(2)}, u32[]{:S(2)}) async-start(bf16[16,128,256]{2,1,0:T(8,128)(2,1)} %copy-done), calls=%async_computation.1 | async-start | bytes 2097152 | tf_op jit(solution)/shard_map/all_to_all | solution.py:368
  72.3 0.8 copy-start.1
  73.1 0.6 copy-start.15
  81.9 4.9 %collective-permute-start = (bf16[16,64,256]{2,1,0:T(8,128)(2,1)}, bf16[16,64,256]{2,1,0:T(8,128)(2,1)S(1)}, u32[]{:S(2)}, u32[]{:S(2)}) collective-permute-start(bf16[16,64,256]{2,1,0:T(8,128)(2,1)} %get-tuple-element.34), channel_id=1, source_target_pairs={{0,16},{16,0},{32,48},{48,32},{64,80},{80,64},{96,112},{112,96},{1... | collective-permute-start | bytes 1572872 | tf_op jit(solution)/shard_map/ppermute | solution.py:457
  89.5 15.2 %all-to-all-start.2 = ((bf16[16,64,256]{2,1,0:T(8,128)(2,1)}), bf16[16,64,256]{2,1,0:T(8,128)(2,1)}, u32[]{:S(2)}, u32[]{:S(2)}) async-start(bf16[16,64,256]{2,1,0:T(8,128)(2,1)} %add_convert_fusion), calls=%async_computation.2 | async-start | bytes 1048576 | tf_op jit(solution)/shard_map/all_to_all | solution.py:368
  93.7 7.2 %copy-start.9 = (f32[256,2048]{1,0:T(8,128)S(1)}, f32[256,2048]{1,0:T(8,128)}, u32[]{:S(2)}) copy-start(f32[256,2048]{1,0:T(8,128)} %copy-done.8) | copy-start | bytes 6291460
  100.9 3.0 %copy-start.2 = (bf16[12,64,256]{2,1,0:T(8,128)(2,1)S(1)}, bf16[12,64,256]{2,1,0:T(8,128)(2,1)}, u32[]{:S(2)}) copy-start(bf16[12,64,256]{2,1,0:T(8,128)(2,1)} %copy-done.1) | copy-start | bytes 1179652
  105.9 8.6 %collective-permute-start.1 = (bf16[64,256]{1,0:T(8,128)(2,1)S(1)}, bf16[64,256]{1,0:T(8,128)(2,1)S(1)}, u32[]{:S(2)}, u32[]{:S(2)}) collective-permute-start(bf16[64,256]{1,0:T(8,128)(2,1)S(1)} %get-tuple-element.40), channel_id=1, source_target_pairs={{0,32},{16,48},{32,0},{48,16},{64,96},{80,112},{96,64},{112,80},{1... | collective-permute-start | bytes 98312 | tf_op jit(solution)/shard_map/ppermute | solution.py:482
  107.9 17.1 %all-to-all-start.3 = ((bf16[16,64,256]{2,1,0:T(8,128)(2,1)}), bf16[16,64,256]{2,1,0:T(8,128)(2,1)S(1)}, u32[]{:S(2)}, u32[]{:S(2)}) async-start(bf16[16,64,256]{2,1,0:T(8,128)(2,1)} %get-tuple-element.41), calls=%async_computation.3 | async-start | bytes 1048576 | tf_op jit(solution)/shard_map/all_to_all | solution.py:368
  114.5 3.8 %collective-permute-start.2 = (bf16[64,256]{1,0:T(8,128)(2,1)S(1)}, bf16[64,256]{1,0:T(8,128)(2,1)S(1)}, u32[]{:S(2)}, u32[]{:S(2)}) collective-permute-start(bf16[64,256]{1,0:T(8,128)(2,1)S(1)} %add_convert_fusion.2), channel_id=1, source_target_pairs={{0,64},{16,80},{32,96},{48,112},{64,0},{80,16},{96,32},{112,48},{1... | collective-permute-start | bytes 98312 | tf_op jit(solution)/shard_map/ppermute | solution.py:482
  118.3 7.8 %collective-permute-start.3 = (bf16[64,256]{1,0:T(8,128)(2,1)S(1)}, bf16[64,256]{1,0:T(8,128)(2,1)S(1)}, u32[]{:S(2)}, u32[]{:S(2)}) collective-permute-start(bf16[64,256]{1,0:T(8,128)(2,1)S(1)} %add_convert_fusion.1.part), channel_id=1, source_target_pairs={{0,128},{16,144},{32,160},{48,176},{64,192},{80,208},{96,224},{112... | collective-permute-start | bytes 98312 | tf_op jit(solution)/shard_map/ppermute | solution.py:485
  141.2 8.1 %collective-permute-start.4 = (bf16[16,64,256]{2,1,0:T(8,128)(2,1)S(1)}, bf16[16,64,256]{2,1,0:T(8,128)(2,1)S(1)}, u32[]{:S(2)}, u32[]{:S(2)}) collective-permute-start(bf16[16,64,256]{2,1,0:T(8,128)(2,1)S(1)} %all_to_all.25.mine), channel_id=1, source_target_pairs={{0,16},{16,0},{32,48},{48,32},{64,80},{80,64},{96,112},{112,96},{1... | collective-permute-start | bytes 1572872 | tf_op jit(solution)/shard_map/ppermute | solution.py:488
